TPU v7x, 256 devices: a whole 4x4x8 slice. The times are simulated.
256 devices in a mesh: pipe: 4 (over z_hi), row: 8 (over z_lo, x), col: 8 (over y, core).
Axes of the slice: x: 4, y: 4, z: 8 (z_hi: 4, z_lo: 2; z = z_hi * 2 + z_lo), core: 2. Of those that a mesh axis runs over, the one named last changes fastest.
Arguments:
- inputs: bfloat16 [4, 2, 512, 4096], P('pipe', None, 'col', 'row'), may hold values from -120 to 120
- grad_out: bfloat16 [2, 512, 4096], P(None, 'col', 'row'), may hold values from -6 to 6
- norm_gain: bfloat16 [4, 4096], P('pipe', 'row'), may hold values from 0.5 to 2
- gate_weight: bfloat16 [4, 4096, 2048], P('pipe', 'col', 'row'), may hold values from -0.25 to 0.25
- up_weight: bfloat16 [4, 4096, 2048], P('pipe', 'col', 'row'), may hold values from -0.25 to 0.25
- down_weight: bfloat16 [4, 4096, 2048], P('pipe', 'col', 'row'), may hold values from -0.25 to 0.25
- inner_cols: int32 [4, 32, 16], P('pipe', None, 'row'), may hold values from 0 to 13, as said below
- inner_counts: int32 [4, 32, 8], P('pipe', None, 'row'), may hold values from 1 to 2, as said below
- outer_cols: int32 [4, 32, 16], P('pipe', None, 'row'), may hold values from 0 to 13, as said below
- outer_counts: int32 [4, 32, 8], P('pipe', None, 'row'), may hold values from 1 to 2, as said below
Outputs:
- grad_in: bfloat16 [4, 2, 512, 4096], P('pipe', None, 'col', 'row')
- grad_gate: bfloat16 [4, 4096, 2048], P('pipe', 'col', 'row')
- grad_up: bfloat16 [4, 4096, 2048], P('pipe', 'col', 'row')
- grad_down: bfloat16 [4, 4096, 2048], P('pipe', 'col', 'row')
Inputs may be any that keep to these rules, and one draw needn't show every extreme that they name: `inner_cols`: within each group of 2 slots of a block row the entries are distinct. `inner_counts`: a slot s of a group is live when s is below the count. `outer_cols`: within each group of 2 slots of a block row the entries are distinct. `outer_counts`: a slot s of a group is live when s is below the count.
All inputs are finite; a program needn't handle non-finite values.
Results may differ from a plain program's by a relative error of at most 0.017.
Values may be sent and summed in bfloat16 or wider, within the bound.
A program may use at most 256 MiB of HBM per device.

v0:
```python
import jax
import jax.numpy as jnp
from jax import lax
from jax.sharding import PartitionSpec as P

FF = 14336
BLK = 128


EPSILON = 1e-05


def passed_along(block, axis, distance):
    devices = range(lax.axis_size(axis))
    route = [(i - distance, i) for i in devices if i - distance in devices]
    return lax.ppermute(block, axis, route)


def block_tables(columns, counts):
    slot_count = columns.shape[1]
    live_slots = (jnp.arange(slot_count, dtype=jnp.int32)[None, :] < counts).astype(jnp.float32)
    return (live_slots, columns.reshape(-1))


def masked_blocks(weight, live_slots):
    row_total = weight.shape[0]
    slot_count = live_slots.shape[1]
    shaped = weight.reshape(row_total // BLK, BLK, slot_count, BLK)
    return jnp.where(live_slots[:, None, :, None] > 0.0, shaped, jnp.zeros_like(shaped))


def spread_blocks(activation, blocks, flat_cols, blocks_local):
    row_count = activation.shape[0]
    block_rows = blocks.shape[0]
    slot_count = blocks.shape[2]
    shaped = activation.reshape(row_count, block_rows, BLK)
    product = jnp.einsum("trk,rksn->rstn", shaped, blocks, preferred_element_type=jnp.float32)
    product = product.reshape(block_rows * slot_count, row_count, BLK)
    return jax.ops.segment_sum(product, flat_cols, num_segments=blocks_local)


def select_blocks(values, flat_cols, picked_shape):
    return jnp.take(values, flat_cols, axis=0).reshape(picked_shape)


def gather_back(picked, blocks):
    result = jnp.einsum("rstn,rksn->trk", picked, blocks, preferred_element_type=jnp.float32)
    return result.reshape(picked.shape[2], -1)


def stored_term(activation_rows, picked, live_slots):
    result = jnp.einsum(
        "mrtk,mrstn->rksn", activation_rows[:, :, 0], picked, preferred_element_type=jnp.float32
    )
    return result * live_slots[:, None, :, None]


def put_slice(buffer_old, new_value, index, active):
    old_slice = lax.dynamic_index_in_dim(buffer_old, index, 0, keepdims=False)
    chosen = jnp.where(active, new_value, old_slice)
    return lax.dynamic_update_index_in_dim(buffer_old, chosen, index, 0)


def local(
    inputs,
    grad_out,
    norm_gain,
    gate_weight,
    up_weight,
    down_weight,
    inner_cols,
    inner_counts,
    outer_cols,
    outer_counts,
):
    phases = lax.axis_size("pipe")
    row_size = lax.axis_size("row")
    phase = lax.axis_index("pipe")
    micro_count = inputs.shape[1]
    token_count = inputs.shape[2]
    part_width = inputs.shape[3]
    full_width = part_width * row_size
    blocks_local = FF // (row_size * BLK)
    gathered_x, gathered_gain = (
        lax.all_gather(inputs, "row", axis=3, tiled=True),
        lax.all_gather(norm_gain, "row", axis=1, tiled=True),
    )
    inputs_full = gathered_x[0].astype(jnp.float32)
    gain_full = gathered_gain[0].astype(jnp.float32)
    inverse_rms = lax.rsqrt(jnp.mean(inputs_full * inputs_full, axis=2) + EPSILON)
    normed = (inputs_full * inverse_rms[:, :, None] * gain_full).astype(jnp.bfloat16)
    inputs_local = inputs[0].astype(jnp.float32)
    gain_local = norm_gain[0].astype(jnp.float32)
    gate_all, up_all, down_all = (
        lax.all_gather(gate_weight, "col", axis=1, tiled=True),
        lax.all_gather(up_weight, "col", axis=1, tiled=True),
        lax.all_gather(down_weight, "col", axis=1, tiled=True),
    )
    inner_live, inner_flat = block_tables(inner_cols[0], inner_counts[0])
    outer_live, outer_flat = block_tables(outer_cols[0], outer_counts[0])
    gate_blocks = masked_blocks(gate_all[0], inner_live)
    up_blocks = masked_blocks(up_all[0], inner_live)
    down_blocks = masked_blocks(down_all[0], outer_live)
    term_shape = gate_blocks.shape
    block_rows = term_shape[0]
    slot_local = term_shape[2]
    picked_shape = (block_rows, slot_local, token_count, BLK)
    rows_shape = (block_rows, 1, token_count, BLK)

    def to_rows(values):
        return values.reshape(token_count, block_rows, BLK).transpose(1, 0, 2)[:, None]

    def layer_front(grad_full, batch_index):
        normed_now = lax.dynamic_index_in_dim(normed, batch_index, 0, keepdims=False)
        gate_pre = spread_blocks(normed_now, gate_blocks, inner_flat, blocks_local)
        up_pre = spread_blocks(normed_now, up_blocks, inner_flat, blocks_local)
        grad_hidden = spread_blocks(grad_full, down_blocks, outer_flat, blocks_local)
        sigmoid = jax.nn.sigmoid(gate_pre)
        hidden = (gate_pre * sigmoid * up_pre).astype(jnp.bfloat16)
        grad_gate = (grad_hidden * up_pre * sigmoid * (1.0 + gate_pre * (1.0 - sigmoid))).astype(
            jnp.bfloat16
        )
        grad_up = (grad_hidden * gate_pre * sigmoid).astype(jnp.bfloat16)
        picked_gate = select_blocks(grad_gate, inner_flat, picked_shape)
        picked_up = select_blocks(grad_up, inner_flat, picked_shape)
        picked_hidden = select_blocks(hidden, outer_flat, picked_shape)
        partial_sum = gather_back(picked_gate, gate_blocks) + gather_back(picked_up, up_blocks)
        extras = (to_rows(grad_full), picked_hidden, picked_gate, picked_up)
        return (partial_sum, extras)

    def layer_blank(grad_full, batch_index):
        blank = jnp.zeros((token_count, full_width), jnp.float32)
        zero_pick = jnp.zeros(picked_shape, jnp.bfloat16)
        extras = (jnp.zeros(rows_shape, jnp.bfloat16), zero_pick, zero_pick, zero_pick)
        return (blank, extras)

    zero_term = jnp.zeros(term_shape, jnp.float32)
    accumulated = (zero_term, zero_term, zero_term)
    store_pick = jnp.zeros((micro_count,) + picked_shape, jnp.bfloat16)
    stored = (
        jnp.zeros((micro_count,) + rows_shape, jnp.bfloat16),
        store_pick,
        store_pick,
        store_pick,
    )
    carried = jnp.zeros((token_count, part_width), jnp.bfloat16)
    grads_in = jnp.zeros((micro_count, token_count, part_width), jnp.bfloat16)
    for moment in range(phases + micro_count - 1):
        batch_index = moment - (phases - 1 - phase)
        active = jnp.logical_and(batch_index >= 0, batch_index < micro_count)
        clamped = jnp.clip(batch_index, 0, micro_count - 1)
        supplied = lax.dynamic_index_in_dim(grad_out, clamped, 0, keepdims=False)
        incoming = jnp.where(phase == phases - 1, supplied, carried)
        grad_full = lax.all_gather(incoming, "row", axis=1, tiled=True)
        partial_sum, extras = lax.cond(active, layer_front, layer_blank, grad_full, clamped)
        inverse_now = lax.dynamic_index_in_dim(inverse_rms, clamped, 0, keepdims=False)
        local_now = lax.dynamic_index_in_dim(inputs_local, clamped, 0, keepdims=False)
        own_share = lax.psum_scatter(partial_sum, "row", scatter_dimension=1, tiled=True)
        statistic = lax.psum(jnp.sum(local_now * gain_local * own_share, axis=1), "row")
        result = incoming.astype(jnp.float32) + gain_local * inverse_now[:, None] * own_share
        result = result - local_now * (inverse_now**3 * statistic / full_width)[:, None]
        result = jnp.where(active, result.astype(jnp.bfloat16), jnp.zeros_like(incoming))
        grads_in = put_slice(grads_in, result, clamped, active)
        stored = jax.tree.map(
            lambda buffer_old, new_value: put_slice(buffer_old, new_value, clamped, active),
            stored,
            extras,
        )
        carried = passed_along(result, "pipe", -1)
    normed_rows = normed.reshape(micro_count, token_count, block_rows, BLK).transpose(0, 2, 1, 3)[
        :, :, None
    ]
    accumulated = (
        stored_term(stored[0], stored[1], outer_live),
        stored_term(normed_rows, stored[2], inner_live),
        stored_term(normed_rows, stored[3], inner_live),
    )
    flat_down, flat_gate, flat_up = jax.tree.map(
        lambda block_sum: block_sum.reshape(full_width, -1), accumulated
    )
    down_sum, gate_sum, up_sum = (
        lax.psum_scatter(flat_down, "col", scatter_dimension=0, tiled=True),
        lax.psum_scatter(flat_gate, "col", scatter_dimension=0, tiled=True),
        lax.psum_scatter(flat_up, "col", scatter_dimension=0, tiled=True),
    )
    return (
        grads_in[None],
        gate_sum.astype(jnp.bfloat16)[None],
        up_sum.astype(jnp.bfloat16)[None],
        down_sum.astype(jnp.bfloat16)[None],
    )


def solution(mesh):
    in_specs = (
        P("pipe", None, "col", "row"),
        P(None, "col", "row"),
        P("pipe", "row"),
        P("pipe", "col", "row"),
        P("pipe", "col", "row"),
        P("pipe", "col", "row"),
        P("pipe", None, "row"),
        P("pipe", None, "row"),
        P("pipe", None, "row"),
        P("pipe", None, "row"),
    )
    out_specs = (
        P("pipe", None, "col", "row"),
        P("pipe", "col", "row"),
        P("pipe", "col", "row"),
        P("pipe", "col", "row"),
    )
    return jax.shard_map(local, mesh=mesh, in_specs=in_specs, out_specs=out_specs, check_vma=False)
```

profile of v0, /device:TPU:1, one launch (start us, length us, event | category | flops | bytes accessed | tf_op | source)
XLA Modules:
  0.0 1041.4 jit_solution(17969161122275750912)
XLA Ops:
  10.0 21.2 %all_gather.33 = bf16[1,4096]{1,0:T(2,128)(2,1)S(1)} all-gather(bf16[1,512]{1,0:T(2,128)(2,1)} %param.24), channel_id=1, replica_groups=mesh['pipe'=4,'row'=8,'col'=8] {'row'}, dimensions={1}, use_global_device_ids=true | all-gather | bytes 9216 | tf_op jit(solution)/shard_map/all_gather | solution.py:86
  36.3 25.7 %all-gather = bf16[1,64,4096]{2,1,0:T(8,128)(2,1)} all-gather(bf16[1,64,512]{2,1,0:T(8,128)(2,1)S(1)} %dynamic-slice_select_fusion), channel_id=2, replica_groups=mesh['pipe'=4,'row'=8,'col'=8] {'row'}, dimensions={2}, use_global_device_ids=true | all-gather | bytes 589824 | tf_op jit(solution)/shard_map/all_gather | solution.py:154
  65.1 19.5 %all-gather.12.cloned.1.call-done = bf16[1,4096,256]{2,1,0:T(8,128)(2,1)} async-done(((bf16[1,512,256]{2,1,0:T(8,128)(2,1)}), bf16[1,4096,256]{2,1,0:T(8,128)(2,1)}) %all-gather.12.cloned.1.call-update) | async-done | bytes 2097168 | tf_op jit(solution)/shard_map/all_gather | solution.py:95
  90.0 24.6 %all-gather.10.cloned.1.call-done = bf16[1,4096,256]{2,1,0:T(8,128)(2,1)} async-done(((bf16[1,512,256]{2,1,0:T(8,128)(2,1)}), bf16[1,4096,256]{2,1,0:T(8,128)(2,1)}) %all-gather.10.cloned.1.call-update) | async-done | bytes 2097168 | tf_op jit(solution)/shard_map/all_gather | solution.py:96
  119.9 24.4 %all-gather.8.cloned.1.call-done = bf16[1,4096,256]{2,1,0:T(8,128)(2,1)} async-done(((bf16[1,512,256]{2,1,0:T(8,128)(2,1)}), bf16[1,4096,256]{2,1,0:T(8,128)(2,1)}) %all-gather.8.cloned.1.call-update) | async-done | bytes 2097168 | tf_op jit(solution)/shard_map/all_gather | solution.py:97
  163.3 91.4 %reduce-scatter.9.cloned.1.call-done = f32[64,512]{1,0:T(8,128)} async-done(((f32[64,4096]{1,0:T(8,128)}), f32[64,512]{1,0:T(8,128)}) %reduce-scatter.9.cloned.1.call-update) | async-done | bytes 131088 | tf_op jit(solution)/shard_map/reduce_scatter | solution.py:158
  256.2 14.4 %psum.35 = f32[64]{0:T(128)} all-reduce(f32[64]{0:T(128)} %fusion.75), channel_id=1, replica_groups=mesh['pipe'=4,'row'=8,'col'=8] {'row'}, use_global_device_ids=true, to_apply=%region_8.10 | all-reduce | flops 64 | bytes 512 | tf_op jit(solution)/shard_map/psum | solution.py:159
  281.3 24.5 %all_gather.36 = bf16[64,4096]{1,0:T(8,128)(2,1)} all-gather(bf16[64,512]{1,0:T(8,128)(2,1)S(1)} %bitcast_select_fusion.22), channel_id=1, replica_groups=mesh['pipe'=4,'row'=8,'col'=8] {'row'}, dimensions={1}, use_global_device_ids=true | all-gather | bytes 589824 | tf_op jit(solution)/shard_map/all_gather | solution.py:154
  312.5 109.3 %reduce-scatter.11.cloned.1.call-done = f32[64,512]{1,0:T(8,128)} async-done(((f32[64,4096]{1,0:T(8,128)}), f32[64,512]{1,0:T(8,128)}) %reduce-scatter.11.cloned.1.call-update) | async-done | bytes 131088 | tf_op jit(solution)/shard_map/reduce_scatter | solution.py:158
  422.9 13.1 %psum.36 = f32[64]{0:T(128)S(1)} all-reduce(f32[64]{0:T(128)S(1)} %fusion.71), channel_id=1, replica_groups=mesh['pipe'=4,'row'=8,'col'=8] {'row'}, use_global_device_ids=true, to_apply=%region_16.18 | all-reduce | flops 64 | bytes 512 | tf_op jit(solution)/shard_map/psum | solution.py:159
  446.3 24.5 %all_gather.37 = bf16[64,4096]{1,0:T(8,128)(2,1)} all-gather(bf16[64,512]{1,0:T(8,128)(2,1)S(1)} %bitcast_select_fusion.20), channel_id=1, replica_groups=mesh['pipe'=4,'row'=8,'col'=8] {'row'}, dimensions={1}, use_global_device_ids=true | all-gather | bytes 589824 | tf_op jit(solution)/shard_map/all_gather | solution.py:154
  484.9 102.4 %reduce-scatter.13.cloned.1.call-done = f32[64,512]{1,0:T(8,128)} async-done(((f32[64,4096]{1,0:T(8,128)}), f32[64,512]{1,0:T(8,128)}) %reduce-scatter.13.cloned.1.call-update) | async-done | bytes 131088 | tf_op jit(solution)/shard_map/reduce_scatter | solution.py:158
  588.9 14.4 %psum.37 = f32[64]{0:T(128)} all-reduce(f32[64]{0:T(128)} %fusion.67), channel_id=1, replica_groups=mesh['pipe'=4,'row'=8,'col'=8] {'row'}, use_global_device_ids=true, to_apply=%region_24.26 | all-reduce | flops 64 | bytes 512 | tf_op jit(solution)/shard_map/psum | solution.py:159
  611.6 24.8 %all_gather.38 = bf16[64,4096]{1,0:T(8,128)(2,1)} all-gather(bf16[64,512]{1,0:T(8,128)(2,1)S(1)} %bitcast_select_fusion.18), channel_id=1, replica_groups=mesh['pipe'=4,'row'=8,'col'=8] {'row'}, dimensions={1}, use_global_device_ids=true | all-gather | bytes 589824 | tf_op jit(solution)/shard_map/all_gather | solution.py:154
  636.5 64.5 %conditional.8 = (f32[64,4096]{1,0:T(8,128)}, bf16[32,1,64,128]{3,0,2,1:T(8,128)(2,1)}, bf16[32,2,64,128]{3,2,1,0:T(8,128)(2,1)}, bf16[32,2,64,128]{3,2,1,0:T(8,128)(2,1)}, bf16[32,2,64,128]{3,2,1,0:T(8,128)(2,1)}) conditional(s32[]{:T(128)} %convert_element_type.177, () %tuple.55, (s32[1,32,2]{1,2,0:T(2,128)}, bf16[64,4096]{1,0:T(8,128)(2,1)}, ...), branch_computations={%region_25.27_spmd, %region_26.31_spmd} | conditional | flops 676334720 | bytes 103339840 | solution.py:155
  713.1 38.4 %reduce-scatter.15.cloned.1.call-done = f32[64,512]{1,0:T(8,128)} async-done(((f32[64,4096]{1,0:T(8,128)}), f32[64,512]{1,0:T(8,128)}) %reduce-scatter.15.cloned.1.call-update) | async-done | bytes 131088 | tf_op jit(solution)/shard_map/reduce_scatter | solution.py:158
  753.0 14.5 %psum.38 = f32[64]{0:T(128)} all-reduce(f32[64]{0:T(128)} %fusion.63), channel_id=1, replica_groups=mesh['pipe'=4,'row'=8,'col'=8] {'row'}, use_global_device_ids=true, to_apply=%region_32.34 | all-reduce | flops 64 | bytes 512 | tf_op jit(solution)/shard_map/psum | solution.py:159
  775.8 24.5 %all_gather.39 = bf16[64,4096]{1,0:T(8,128)(2,1)} all-gather(bf16[64,512]{1,0:T(8,128)(2,1)S(1)} %bitcast_select_fusion.16), channel_id=1, replica_groups=mesh['pipe'=4,'row'=8,'col'=8] {'row'}, dimensions={1}, use_global_device_ids=true | all-gather | bytes 589824 | tf_op jit(solution)/shard_map/all_gather | solution.py:154
  800.3 56.5 %conditional.9 = (f32[64,4096]{1,0:T(8,128)}, bf16[32,1,64,128]{3,0,2,1:T(8,128)(2,1)S(1)}, bf16[32,2,64,128]{3,2,1,0:T(8,128)(2,1)}, bf16[32,2,64,128]{3,2,1,0:T(8,128)(2,1)}, bf16[32,2,64,128]{3,2,1,0:T(8,128)(2,1)}) conditional(s32[]{:T(128)} %convert_element_type.180, () %tuple.57, (s32[1,32,2]{1,2,0:T(2,128)}, bf16[64,4096]{1,0:T(8,128)(2,1)}, ...), branch_computations={%region_33.35_spmd, %region_34.39_spmd} | conditional | flops 676334720 | bytes 107792528 | solution.py:155
  896.1 8.0 copy.367
  920.0 8.1 copy.368
  930.0 14.1 %psum.39 = f32[64]{0:T(128)S(1)} all-reduce(f32[64]{0:T(128)S(1)} %fusion.59), channel_id=1, replica_groups=mesh['pipe'=4,'row'=8,'col'=8] {'row'}, use_global_device_ids=true, to_apply=%region_40.42 | all-reduce | flops 64 | bytes 512 | tf_op jit(solution)/shard_map/psum | solution.py:159
  950.8 40.0 %reduce-scatter.21.cloned.1.call-done = f32[512,256]{0,1:T(8,128)} async-done(((f32[4096,256]{0,1:T(8,128)}), f32[512,256]{0,1:T(8,128)}) %reduce-scatter.21.cloned.1.call-update) | async-done | bytes 524304 | tf_op jit(solution)/shard_map/reduce_scatter | solution.py:184
  992.6 39.8 %reduce-scatter.19.cloned.1.call-done = f32[512,256]{0,1:T(8,128)} async-done(((f32[4096,256]{0,1:T(8,128)}), f32[512,256]{0,1:T(8,128)}) %reduce-scatter.19.cloned.1.call-update) | async-done | bytes 524304 | tf_op jit(solution)/shard_map/reduce_scatter | solution.py:183
  (374 shorter events, 321.0 us)
Async XLA Ops:
  7.2 54.8 %all-gather.6.cloned.1.call-start = ((), (), s32[]{:S(2)}) async-start(), calls=%async_computation.8 | async-start | bytes 1179648 | tf_op jit(solution)/shard_map/all_gather | solution.py:85
  7.9 76.7 %all-gather.12.cloned.1.call-start = ((), (), s32[]{:S(2)}) async-start(), calls=%async_computation.11 | async-start | bytes 2359296 | tf_op jit(solution)/shard_map/all_gather | solution.py:95
  8.6 105.9 %all-gather.10.cloned.1.call-start = ((), (), s32[]{:S(2)}) async-start(), calls=%async_computation.10 | async-start | bytes 2359296 | tf_op jit(solution)/shard_map/all_gather | solution.py:96
  9.4 134.9 %all-gather.8.cloned.1.call-start = ((), (), s32[]{:S(2)}) async-start(), calls=%async_computation.9 | async-start | bytes 2359296 | tf_op jit(solution)/shard_map/all_gather | solution.py:97
  10.0 244.7 %reduce-scatter.9.cloned.1.call-start = ((), (), s32[]{:S(2)}) async-start(), calls=%async_computation.12 | async-start | bytes 1179648 | tf_op jit(solution)/shard_map/reduce_scatter | solution.py:158
  160.8 145.0 %copy-start.26 = (bf16[2,64,4096]{2,1,0:T(8,128)(2,1)S(1)}, bf16[2,64,4096]{2,1,0:T(8,128)(2,1)}, u32[]{:S(2)}) copy-start(bf16[2,64,4096]{2,1,0:T(8,128)(2,1)} %copy-done.25) | copy-start | bytes 3145732
  160.8 261.0 %reduce-scatter.11.cloned.1.call-start = ((), (), s32[]{:S(2)}) async-start(), calls=%async_computation.13 | async-start | bytes 1179648 | tf_op jit(solution)/shard_map/reduce_scatter | solution.py:158
  163.3 142.5 %copy-start.31 = (f32[1,2,64,512]{3,2,1,0:T(8,128)}, f32[1,2,64,512]{3,2,1,0:T(8,128)S(1)}, u32[]{:S(2)}) copy-start(f32[1,2,64,512]{3,2,1,0:T(8,128)S(1)} %convert_element_type.168) | copy-start | bytes 786436
  273.6 6.2 collective-permute-start
  311.5 159.3 %copy-start.27 = (bf16[2,64,4096]{2,1,0:T(8,128)(2,1)S(1)}, bf16[2,64,4096]{2,1,0:T(8,128)(2,1)}, u32[]{:S(2)}) copy-start(bf16[2,64,4096]{2,1,0:T(8,128)(2,1)} %copy-done.25) | copy-start | bytes 3145732
  311.5 159.3 %copy-start.75 = (s32[64]{0:T(128)S(1)}, s32[64]{0:T(128)}, u32[]{:S(2)}) copy-start(s32[64]{0:T(128)} %copy-done.74) | copy-start | bytes 772
  311.5 159.3 %copy-start.80 = (s32[64]{0:T(128)S(1)}, s32[64]{0:T(128)}, u32[]{:S(2)}) copy-start(s32[64]{0:T(128)} %copy-done.79) | copy-start | bytes 772
  311.5 159.3 %copy-start.87 = (s32[1,32,2]{1,2,0:T(2,128)S(1)}, s32[1,32,2]{1,2,0:T(2,128)}, u32[]{:S(2)}) copy-start(s32[1,32,2]{1,2,0:T(2,128)} %param.30) | copy-start | bytes 772
  311.5 159.3 %copy-start.92 = (s32[1,32,2]{1,2,0:T(2,128)S(1)}, s32[1,32,2]{1,2,0:T(2,128)}, u32[]{:S(2)}) copy-start(s32[1,32,2]{1,2,0:T(2,128)} %param.28) | copy-start | bytes 772
  311.5 275.8 %reduce-scatter.13.cloned.1.call-start = ((), (), s32[]{:S(2)}) async-start(), calls=%async_computation.14 | async-start | bytes 1179648 | tf_op jit(solution)/shard_map/reduce_scatter | solution.py:158
  438.4 6.5 collective-permute-start.1
  477.0 274.5 %reduce-scatter.15.cloned.1.call-start = ((), (), s32[]{:S(2)}) async-start(), calls=%async_computation.15 | async-start | bytes 1179648 | tf_op jit(solution)/shard_map/reduce_scatter | solution.py:158
  483.4 153.1 %copy-start.21 = (bf16[2,32,1,64,128]{4,3,0,1,2:T(8,128)(2,1)}, bf16[2,32,1,64,128]{4,3,0,1,2:T(8,128)(2,1)S(1)}, u32[]{:S(2)}) copy-start(bf16[2,32,1,64,128]{4,3,0,1,2:T(8,128)(2,1)S(1)} %copy_dynamic-update-slice_fusion.4) | copy-start | bytes 3145732
  605.7 5.9 collective-permute-start.2
  701.0 228.0 %reduce-scatter.17.cloned.1.call-start = ((), (), s32[]{:S(2)}) async-start(), calls=%async_computation.16 | async-start | bytes 1179648 | tf_op jit(solution)/shard_map/reduce_scatter | solution.py:158
  769.9 5.9 collective-permute-start.3
  857.6 91.3 %reduce-scatter.23.cloned.1.call-start = ((), (), s32[]{:S(2)}) async-start(), calls=%async_computation.19 | async-start | bytes 4718592 | tf_op jit(solution)/shard_map/reduce_scatter | solution.py:182
  880.6 110.1 %reduce-scatter.21.cloned.1.call-start = ((), (), s32[]{:S(2)}) async-start(), calls=%async_computation.18 | async-start | bytes 4718592 | tf_op jit(solution)/shard_map/reduce_scatter | solution.py:184
  904.2 128.2 %reduce-scatter.19.cloned.1.call-start = ((), (), s32[]{:S(2)}) async-start(), calls=%async_computation.17 | async-start | bytes 4718592 | tf_op jit(solution)/shard_map/reduce_scatter | solution.py:183
  (69 other events, 1236.5 us)
Sparse Core Ops, SparseCore 0:
  9.8 40.5 all-gather.5
  52.3 32.2 all-gather.11
  86.4 28.0 all-gather.9
  116.2 28.0 all-gather.7
  160.9 93.7 reduce-scatter.8
  311.7 110.1 reduce-scatter.10
  477.1 110.2 reduce-scatter.12
  701.1 50.2 reduce-scatter.14
  857.7 47.3 reduce-scatter.16
  907.5 41.2 reduce-scatter.22
  951.4 39.2 reduce-scatter.20
  993.1 39.3 reduce-scatter.18
where the time goes:
time: 1060 us; the launch traced here: 1040 us
  waiting for transfers between devices  514 us (48%)
  blocking collectives  216 us (20%)
  local copies, waits for them, and re-layouts  137 us (13%)
  other arithmetic  113 us (11%)
  matrix products  39.5 us (4%)
  between operations  15.3 us (1%)
    reduce_scatter x5, waiting for transfers between devices, local(): lax.psum_scatter(partial_sum, 'row', scatter_dimension=1, tiled=True)  342 us
    all_gather x5, blocking collectives, local(): grad_full = lax.all_gather(incoming, 'row', axis=1, tiled=True)  124 us
    psum x5, blocking collectives, local(): lax.psum(jnp.sum(local_now * gain_local * own_share, axis=1), 'row')  70.6 us
    scatter-add x6, other arithmetic, spread_blocks(): return jax.ops.segment_sum(product, flat_cols, num_segments=blocks_local)  42.3 us
    reduce_scatter x1, waiting for transfers between devices, local(): lax.psum_scatter(flat_up, 'col', scatter_dimension=0, tiled=True)  40 us
    reduce_scatter x1, waiting for transfers between devices, local(): lax.psum_scatter(flat_gate, 'col', scatter_dimension=0, tiled=True)  39.8 us
    unnamed x108, local copies, waits for them, and re-layouts  34.6 us
    another operation x29, local copies, waits for them, and re-layouts  33.5 us
  transfers between devices with their start and end apart: 16, of which 14 were waited for; matrix products, arithmetic and copies ran while one was open for 11% of the time, Pallas kernels for 0%

commit v1 on v0

v1 whole, which is shorter than its diff:
```python
import functools

import jax
import jax.numpy as jnp
from jax import lax
from jax.experimental import pallas as pl
from jax.experimental.pallas import tpu as pltpu
from jax.sharding import PartitionSpec as P

FF = 14336
BLK = 128
EPSILON = 1e-05
MESH = pl.DeviceIdType.MESH
F32 = jnp.float32
BF16 = jnp.bfloat16


def sort_kernel(blocks, icol, ocol, iord, ikeep, iend, ihas, oord, okeep, oend, ohas, start):
    slots = icol.shape[0]
    for col, order, keep, end, has in ((icol, iord, ikeep, iend, ihas), (ocol, oord, okeep, oend, ohas)):

        def clear(j, _):
            start[j] = 0
            return 0

        lax.fori_loop(0, blocks + 1, clear, 0)

        def count(k, _, col=col):
            start[col[k] + 1] = start[col[k] + 1] + 1
            return 0

        lax.fori_loop(0, slots, count, 0)

        def total(j, _, has=has):
            has[j] = jnp.minimum(start[j + 1], 1).astype(F32)
            start[j + 1] = start[j + 1] + start[j]
            return 0

        lax.fori_loop(0, blocks, total, 0)

        def place(k, _, col=col, order=order, end=end):
            at = start[col[k]]
            order[at] = k
            start[col[k]] = at + 1
            end[col[k]] = at
            return 0

        def last(j, _, end=end):
            end[j] = 0
            return 0

        lax.fori_loop(0, blocks, last, 0)
        lax.fori_loop(0, slots, place, 0)
        keep[0] = 0.0

        def same(i, _, col=col, order=order, keep=keep):
            keep[i] = jnp.where(col[order[i]] == col[order[i - 1]], 1.0, 0.0).astype(F32)
            return 0

        lax.fori_loop(1, slots, same, 0)


def dot(a, b):
    return jnp.dot(a, b, preferred_element_type=F32)


def dot_nt(a, b):
    return lax.dot_general(a, b, (((1,), (1,)), ((), ())), preferred_element_type=F32)


def main_kernel(
    sizes,
    x_ref, go_ref, gain_ref, gate_ref, up_ref, down_ref,
    icol, icnt, ocol, ocnt,
    iord, ikeep, iend, ihas, oord, okeep, oend, ohas,
    gin_ref, ggate_ref, gup_ref, gdown_ref,
    wall, xg, xn, xnt, rinv, pg, pu, sg, su, ab, bb, cb, hb, dgb, dub, dyg, rss, rsr, ds, dr, ys, yr, own,
    wsend, wrecv, xsend, xrecv, gsend, grecv, hsend, hrecv, rsend, rrecv, dsend, drecv, ysend, yrecv,
):
    n_pipe, n_row, n_y, blocks = sizes
    micro, tokens, width = go_ref.shape
    both = micro * tokens
    features = width * n_row
    block_rows = features // BLK
    per_row = block_rows // n_row
    per_col = block_rows // (2 * n_y)
    slots = 2 * block_rows
    half = per_col * 3 * BLK // 2

    p = lax.axis_index("pipe")
    r = lax.axis_index("row")
    c = lax.axis_index("col")
    y = lax.div(c, 2)
    core = lax.rem(c, 2)

    def column(dy, dcore):
        return lax.rem(y + dy, n_y) * 2 + lax.rem(core + dcore, 2)

    up_y, down_y, far_y, sibling = column(1, 0), column(n_y - 1, 0), column(2, 0), column(0, 1)

    def rows_of(block, which):
        return pl.ds((block * 3 + which) * BLK, BLK)

    barrier = pltpu.get_barrier_semaphore()

    def greet(d, _):
        pl.semaphore_signal(barrier, inc=1, device_id={"row": lax.rem(r + d, n_row)}, device_id_type=MESH)
        return 0

    lax.fori_loop(1, n_row, greet, 0)
    for other in (up_y, down_y, far_y, sibling):
        pl.semaphore_signal(barrier, inc=1, device_id={"col": other}, device_id_type=MESH)

    @pl.when(p > 0)
    def _():
        pl.semaphore_signal(barrier, inc=1, device_id={"pipe": p - 1}, device_id_type=MESH)

    @pl.when(p < n_pipe - 1)
    def _():
        pl.semaphore_signal(barrier, inc=1, device_id={"pipe": p + 1}, device_id_type=MESH)

    xg[r, 0:both, :] = x_ref[...]
    xg[r, both : both + 16, :] = jnp.broadcast_to(gain_ref[...].astype(F32), (16, width)).astype(BF16)
    for i in range(per_col):
        for which, (ref, cnt) in enumerate(((gate_ref, icnt), (up_ref, icnt), (down_ref, ocnt))):
            live = cnt[c * per_col + i]
            shape = (BLK, 2 * BLK)
            slot = lax.broadcasted_iota(jnp.int32, shape, 1) // BLK
            value = ref[i * BLK : (i + 1) * BLK, :].astype(F32)
            wall[c, rows_of(i, which), :] = jnp.where(slot < live, value, 0.0).astype(BF16)

    @pl.when(p == n_pipe - 1)
    def _():
        for m in range(micro):
            dyg[m, r] = go_ref[m]

    pl.semaphore_wait(barrier, n_row + 3 + jnp.where(p > 0, 1, 0) + jnp.where(p < n_pipe - 1, 1, 0))

    def weights(owner, h, target, number):
        piece = wall.at[owner, pl.ds(h * half, half), :]
        return pltpu.make_async_remote_copy(
            src_ref=piece, dst_ref=piece, send_sem=wsend.at[number], recv_sem=wrecv.at[owner, h],
            device_id={"col": target}, device_id_type=MESH,
        )

    def x_copy(owner, target, number):
        return pltpu.make_async_remote_copy(
            src_ref=xg.at[owner], dst_ref=xg.at[owner], send_sem=xsend.at[number], recv_sem=xrecv.at[owner],
            device_id={"row": target}, device_id_type=MESH,
        )

    def dy_copy(m, owner, target, number):
        piece = dyg.at[m, owner]
        return pltpu.make_async_remote_copy(
            src_ref=piece, dst_ref=piece, send_sem=gsend.at[m, number], recv_sem=grecv.at[m, owner],
            device_id={"row": target}, device_id_type=MESH,
        )

    def hop_copy(m, target):
        return pltpu.make_async_remote_copy(
            src_ref=gin_ref.at[m], dst_ref=dyg.at[m, r], send_sem=hsend.at[m], recv_sem=hrecv.at[m],
            device_id={"pipe": target}, device_id_type=MESH,
        )

    def sum_copy(m, target, source, number):
        return pltpu.make_async_remote_copy(
            src_ref=rss.at[m, target], dst_ref=rsr.at[m, source], send_sem=rsend.at[m, number], recv_sem=rrecv.at[m, source],
            device_id={"row": target}, device_id_type=MESH,
        )

    def pair_copy(which, k):
        return pltpu.make_async_remote_copy(
            src_ref=ds.at[which, k], dst_ref=dr.at[which, k], send_sem=dsend.at[which, k], recv_sem=drecv.at[which, k],
            device_id={"col": sibling}, device_id_type=MESH,
        )

    def ring_copy(which, k, target):
        return pltpu.make_async_remote_copy(
            src_ref=ys.at[which, k], dst_ref=yr.at[which, k], send_sem=ysend.at[which, k], recv_sem=yrecv.at[which, k],
            device_id={"col": target}, device_id_type=MESH,
        )

    def send_dy(m):
        def body(d, _):
            dy_copy(m, r, lax.rem(r + d, n_row), d).start()
            return 0

        lax.fori_loop(1, n_row, body, 0)

    def send_x(d, _):
        x_copy(r, lax.rem(r + d, n_row), d).start()
        return 0

    lax.fori_loop(1, n_row, send_x, 0)
    weights(c, 0, up_y, 0).start()
    weights(c, 1, down_y, 1).start()
    weights(c, 1, up_y, 2).start()
    weights(c, 0, down_y, 3).start()
    weights(c, 0, sibling, 4).start()
    weights(c, 1, sibling, 5).start()

    @pl.when(p == n_pipe - 1)
    def _():
        for m in range(micro):
            send_dy(m)

    rinv[...] = jnp.zeros_like(rinv)

    def squares(d, _):
        owner = lax.rem(r + d, n_row)

        @pl.when(d > 0)
        def _():
            x_copy(owner, owner, 0).wait_recv()

        total = rinv[...]
        for i in range(per_row):
            value = xg[owner, 0:both, i * BLK : (i + 1) * BLK].astype(F32)
            total = total + value * value
        rinv[...] = total
        return 0

    lax.fori_loop(0, n_row, squares, 0)
    mean = jnp.sum(rinv[...], axis=1, keepdims=True) / features
    rinv[...] = jnp.broadcast_to(lax.rsqrt(mean + EPSILON), (both, BLK))

    def norm(owner, _):
        scale = rinv[...]
        for i in range(per_row):
            lanes = slice(i * BLK, (i + 1) * BLK)
            gain = xg[owner, both : both + 16, lanes].astype(F32)[0:1, :]
            value = xg[owner, 0:both, lanes].astype(F32)
            xn[owner * per_row + i] = (value * scale * gain).astype(BF16)
        return 0

    lax.fori_loop(0, n_row, norm, 0)

    def arrive(k, _):
        @pl.when(k == 1)
        def _():
            for h in range(2):
                weights(sibling, h, sibling, 0).wait_recv()

        @pl.when(k == 2)
        def _():
            weights(down_y, 0, sibling, 0).wait_recv()
            weights(down_y, 0, up_y, 6).start()
            weights(down_y, 0, sibling, 7).start()
            weights(up_y, 1, sibling, 0).wait_recv()
            weights(up_y, 1, down_y, 8).start()
            weights(up_y, 1, sibling, 9).start()
            weights(down_y, 1, sibling, 0).wait_recv()
            weights(down_y, 1, sibling, 10).start()

        @pl.when(k == 3)
        def _():
            weights(up_y, 0, sibling, 0).wait_recv()
            weights(up_y, 0, sibling, 11).start()

        @pl.when(k == 4)
        def _():
            for h in range(2):
                weights(column(n_y - 1, 1), h, sibling, 0).wait_recv()

        @pl.when(k == 5)
        def _():
            for h in range(2):
                weights(column(1, 1), h, sibling, 0).wait_recv()

        @pl.when(k == 6)
        def _():
            for h in range(2):
                weights(far_y, h, sibling, 0).wait_recv()
                weights(far_y, h, sibling, 12 + h).start()

        @pl.when(k == 7)
        def _():
            for h in range(2):
                weights(column(2, 1), h, sibling, 0).wait_recv()

        turn = jnp.where(k < 2, 0, jnp.where(k >= 6, 2, jnp.where(lax.rem(k, 2) == 0, n_y - 1, 1)))
        other = jnp.where(jnp.logical_or(k == 1, jnp.logical_or(k == 4, jnp.logical_or(k == 5, k == 7))), 1, 0)
        owner = column(turn, other)
        for i in range(per_col):
            block_row = owner * per_col + i
            value = xn[block_row]
            for which, out in ((0, pg), (1, pu)):
                product = dot(value, wall[owner, rows_of(i, which), :])
                out[2 * block_row] = product[:, :BLK]
                out[2 * block_row + 1] = product[:, BLK:]
        return 0

    lax.fori_loop(0, 2 * n_y, arrive, 0)

    def add_slots(order, keep, source, out, rows):
        def body(i, total):
            total = total * keep[i] + source[order[i], 0:rows, :]
            out[i, 0:rows, :] = total
            return total

        lax.fori_loop(0, slots, body, jnp.zeros((rows, BLK), F32), unroll=4)

    add_slots(iord, ikeep, pg, sg, both)
    add_slots(iord, ikeep, pu, su, both)

    def hidden(j, _):
        g = sg[iend[j]] * ihas[j]
        u = su[iend[j]] * ihas[j]
        s = jax.nn.sigmoid(g)
        a = u * s * (1.0 + g * (1.0 - s))
        b = g * s
        h = (b * u).astype(BF16)
        e = a * g + b * u
        for m in range(micro):
            part = slice(m * tokens, (m + 1) * tokens)
            ab[m, j] = a[part]
            bb[m, j] = b[part]
            cb[m, j] = e[part]
            hb[m, j] = h[part]
        return 0

    lax.fori_loop(0, blocks, hidden, 0)

    def stacked(ref, j):
        return jnp.concatenate([ref[m, j] for m in range(micro)], axis=0)

    def grads(owner, emit):
        for i in range(per_col):
            block_row = owner * per_col + i
            row_owner = lax.div(block_row, per_row)
            place = lax.rem(block_row, per_row)
            rows = slice(i * BLK, (i + 1) * BLK)
            j0, j1 = icol[2 * block_row], icol[2 * block_row + 1]
            q0, q1 = ocol[2 * block_row], ocol[2 * block_row + 1]
            lanes = pl.ds(pl.multiple_of(place * BLK, BLK), BLK)
            dy = jnp.concatenate([dyg[m, row_owner, :, lanes] for m in range(micro)], axis=0)
            emit(2, rows, dot(dy.T, jnp.concatenate([stacked(hb, q0), stacked(hb, q1)], axis=1)))
            left = xnt[block_row]
            emit(0, rows, dot(left, jnp.concatenate([stacked(dgb, j0), stacked(dgb, j1)], axis=1)))
            emit(1, rows, dot(left, jnp.concatenate([stacked(dub, j0), stacked(dub, j1)], axis=1)))

    def grads_sibling():
        def body(k, _):
            def emit(which, rows, value):
                ds[which, k, rows, :] = value.astype(BF16)

            grads(lax.rem(y + k, n_y) * 2 + (1 - core), emit)
            for which in range(3):
                pair_copy(which, k).start()
            return 0

        lax.fori_loop(0, n_y, body, 0)

    def front(m):
        def products(d, _):
            owner = lax.rem(r + d, n_row)

            @pl.when(d > 0)
            def _():
                dy_copy(m, owner, owner, 0).wait_recv()

            for i in range(per_row):
                block_row = owner * per_row + i
                col_owner = lax.div(block_row, per_col)
                place = lax.rem(block_row, per_col)
                rows = pl.ds(pl.multiple_of((place * 3 + 2) * BLK, BLK), BLK)
                product = dot(dyg[m, owner, :, i * BLK : (i + 1) * BLK], wall[col_owner, rows, :])
                pg[2 * block_row, 0:tokens, :] = product[:, :BLK]
                pg[2 * block_row + 1, 0:tokens, :] = product[:, BLK:]
            return 0

        lax.fori_loop(0, n_row, products, 0)
        add_slots(oord, okeep, pg, sg, tokens)

        def gated(j, total):
            dh = sg[oend[j], 0:tokens, :] * ohas[j]
            dgb[m, j] = (dh * ab[m, j]).astype(BF16)
            dub[m, j] = (dh * bb[m, j]).astype(BF16)
            return total + dh * cb[m, j]

        total = lax.fori_loop(0, blocks, gated, jnp.zeros((tokens, BLK), F32))
        stat = jnp.sum(total, axis=1, keepdims=True)
        high = stat.astype(BF16).astype(F32)
        lane = lax.broadcasted_iota(jnp.int32, (tokens, BLK), 1)
        stat = jnp.where(lane < BLK // 2, high, stat - high).astype(BF16)

        def back(d, _):
            owner = lax.rem(r + d, n_row)
            for i in range(per_row):
                block_row = owner * per_row + i
                col_owner = lax.div(block_row, per_col)
                place = lax.rem(block_row, per_col)
                j0, j1 = icol[2 * block_row], icol[2 * block_row + 1]
                rows = pl.ds(pl.multiple_of(place * 3 * BLK, BLK), BLK)
                part = dot_nt(jnp.concatenate([dgb[m, j0], dgb[m, j1]], axis=1), wall[col_owner, rows, :])
                rows = pl.ds(pl.multiple_of((place * 3 + 1) * BLK, BLK), BLK)
                part = part + dot_nt(jnp.concatenate([dub[m, j0], dub[m, j1]], axis=1), wall[col_owner, rows, :])
                rss[m, owner, :, i * BLK : (i + 1) * BLK] = part.astype(BF16)
            rss[m, owner, :, width : width + BLK] = stat

            @pl.when(d < n_row)
            def _():
                sum_copy(m, owner, r, d).start()

            return 0

        lax.fori_loop(1, n_row + 1, back, 0)

    def finish(m):
        tile = pl.ds(pl.multiple_of(m * tokens, tokens), tokens)

        def body(d, total):
            owner = lax.rem(r + d, n_row)
            sum_copy(m, owner, owner, 0).wait_recv()
            return total + rsr[m, owner].astype(F32)

        total = lax.fori_loop(1, n_row, body, rss[m, r].astype(F32))
        stat = jnp.sum(total[:, width:], axis=1, keepdims=True) / (BLK // 2)
        scale = rinv[tile, :][:, 0:1]
        gain = xg[r, both : both + 16, :].astype(F32)[0:1, :]
        value = xg[r, tile, :].astype(F32)
        result = dyg[m, r].astype(F32) + gain * scale * total[:, :width]
        result = result - value * (scale * scale * stat / features)
        gin_ref[m] = result.astype(BF16)

        @pl.when(p > 0)
        def _():
            hop_copy(m, p - 1).start()

    def take_dy(m):
        @pl.when(p < n_pipe - 1)
        def _():
            hop_copy(m, p + 1).wait_recv()
            send_dy(m)

    take_dy(0)

    def chain(m, _):
        front(m)

        @pl.when(m == 0)
        def _():
            take_dy(1)

            def turn(b, _):
                xnt[b] = xn[b].T
                return 0

            lax.fori_loop(0, block_rows, turn, 0)

        @pl.when(jnp.logical_and(m == micro - 1, p == 0))
        def _():
            grads_sibling()

        finish(m)
        return 0

    lax.fori_loop(0, micro, chain, 0)

    @pl.when(p > 0)
    def _():
        grads_sibling()

    def grads_ring(step, _):
        k = lax.rem(step + 2, n_y)
        target = lax.rem(y + k, n_y) * 2 + core
        for which in range(3):
            pair_copy(which, k).wait_recv()

        def emit(which, rows, value):
            value = value + dr[which, k, rows, :].astype(F32)
            own[which, rows, :] = value
            ys[which, k, rows, :] = value.astype(BF16)

        grads(target, emit)

        @pl.when(k > 0)
        def _():
            for which in range(3):
                ring_copy(which, k, target).start()

        return 0

    def ring_order(step, _):
        return grads_ring(jnp.where(step == 0, 0, jnp.where(step == 1, 1, jnp.where(step == 2, 3, 2))), 0)

    lax.fori_loop(0, n_y, ring_order, 0)

    def collect(k, _):
        for which in range(3):
            ring_copy(which, k, sibling).wait_recv()
            own[which] = own[which] + yr[which, k].astype(F32)
        return 0

    lax.fori_loop(1, n_y, collect, 0)
    for i in range(per_col):
        for which, (ref, cnt) in enumerate(((ggate_ref, icnt), (gup_ref, icnt), (gdown_ref, ocnt))):
            live = cnt[c * per_col + i]
            slot = lax.broadcasted_iota(jnp.int32, (BLK, 2 * BLK), 1) // BLK
            rows = slice(i * BLK, (i + 1) * BLK)
            ref[rows, :] = jnp.where(slot < live, own[which, rows, :], 0.0).astype(BF16)

    for number in range(14):
        weights(c, 0, sibling, number).wait_send()

    def sent(d, _):
        other = lax.rem(r + d, n_row)
        x_copy(r, other, d).wait_send()
        for m in range(micro):
            dy_copy(m, r, other, d).wait_send()
            sum_copy(m, other, r, d).wait_send()
        return 0

    lax.fori_loop(1, n_row, sent, 0)

    @pl.when(p > 0)
    def _():
        for m in range(micro):
            hop_copy(m, p - 1).wait_send()

    for which in range(3):
        for k in range(n_y):
            pair_copy(which, k).wait_send()
            if k > 0:
                ring_copy(which, k, sibling).wait_send()


def local(sizes, inputs, grad_out, norm_gain, gate_weight, up_weight, down_weight, inner_cols, inner_counts, outer_cols, outer_counts):
    n_pipe, n_row, n_y, blocks = sizes
    _, micro, tokens, width = inputs.shape
    both = micro * tokens
    block_rows = width * n_row // BLK
    slots = 2 * block_rows
    rows = gate_weight.shape[1]
    icol, ocol = inner_cols.reshape(slots), outer_cols.reshape(slots)
    icnt, ocnt = inner_counts.reshape(block_rows), outer_counts.reshape(block_rows)
    smem = pl.BlockSpec(memory_space=pltpu.SMEM)
    vmem = pl.BlockSpec(memory_space=pltpu.VMEM)
    table = (
        jax.ShapeDtypeStruct((slots,), jnp.int32),
        jax.ShapeDtypeStruct((slots,), F32),
        jax.ShapeDtypeStruct((blocks,), jnp.int32),
        jax.ShapeDtypeStruct((blocks,), F32),
    )
    tables = pl.pallas_call(
        functools.partial(sort_kernel, blocks),
        out_shape=table + table,
        in_specs=[smem, smem],
        out_specs=[smem] * 8,
        scratch_shapes=[pltpu.SMEM((blocks + 1,), jnp.int32)],
        name="order_slots",
    )(icol, ocol)
    dma = pltpu.SemaphoreType.DMA
    weight_out = jax.ShapeDtypeStruct((rows, 2 * BLK), BF16)
    grad_in, gate, up, down = pl.pallas_call(
        functools.partial(main_kernel, sizes),
        out_shape=(jax.ShapeDtypeStruct((micro, tokens, width), BF16), weight_out, weight_out, weight_out),
        in_specs=[vmem] * 6 + [smem] * 12,
        out_specs=[vmem] * 4,
        scratch_shapes=[
            pltpu.VMEM((2 * n_y, 3 * rows, 2 * BLK), BF16),
            pltpu.VMEM((n_row, both + 16, width), BF16),
            pltpu.VMEM((block_rows, both, BLK), BF16),
            pltpu.VMEM((block_rows, BLK, both), BF16),
            pltpu.VMEM((both, BLK), F32),
            pltpu.VMEM((slots, both, BLK), F32),
            pltpu.VMEM((slots, both, BLK), F32),
            pltpu.VMEM((slots, both, BLK), F32),
            pltpu.VMEM((slots, both, BLK), F32),
            pltpu.VMEM((micro, blocks, tokens, BLK), F32),
            pltpu.VMEM((micro, blocks, tokens, BLK), F32),
            pltpu.VMEM((micro, blocks, tokens, BLK), F32),
            pltpu.VMEM((micro, blocks, tokens, BLK), BF16),
            pltpu.VMEM((micro, blocks, tokens, BLK), BF16),
            pltpu.VMEM((micro, blocks, tokens, BLK), BF16),
            pltpu.VMEM((micro, n_row, tokens, width), BF16),
            pltpu.VMEM((micro, n_row, tokens, width + BLK), BF16),
            pltpu.VMEM((micro, n_row, tokens, width + BLK), BF16),
            pltpu.VMEM((3, n_y, rows, 2 * BLK), BF16),
            pltpu.VMEM((3, n_y, rows, 2 * BLK), BF16),
            pltpu.VMEM((3, n_y, rows, 2 * BLK), BF16),
            pltpu.VMEM((3, n_y, rows, 2 * BLK), BF16),
            pltpu.VMEM((3, rows, 2 * BLK), F32),
            dma((14,)), dma((2 * n_y, 2)),
            dma((n_row,)), dma((n_row,)),
            dma((micro, n_row)), dma((micro, n_row)),
            dma((micro,)), dma((micro,)),
            dma((micro, n_row)), dma((micro, n_row)),
            dma((3, n_y)), dma((3, n_y)),
            dma((3, n_y)), dma((3, n_y)),
        ],
        compiler_params=pltpu.CompilerParams(collective_id=0, has_side_effects=True, vmem_limit_bytes=56 * 1024 * 1024),
        name="backward",
    )(
        inputs.reshape(both, width), grad_out, norm_gain,
        gate_weight.reshape(rows, 2 * BLK), up_weight.reshape(rows, 2 * BLK), down_weight.reshape(rows, 2 * BLK),
        icol, icnt, ocol, ocnt, *tables,
    )
    return grad_in[None], gate[None], up[None], down[None]


def solution(mesh):
    in_specs = (
        P("pipe", None, "col", "row"),
        P(None, "col", "row"),
        P("pipe", "row"),
        P("pipe", "col", "row"),
        P("pipe", "col", "row"),
        P("pipe", "col", "row"),
        P("pipe", None, "row"),
        P("pipe", None, "row"),
        P("pipe", None, "row"),
        P("pipe", None, "row"),
    )
    out_specs = (
        P("pipe", None, "col", "row"),
        P("pipe", "col", "row"),
        P("pipe", "col", "row"),
        P("pipe", "col", "row"),
    )
    sizes = (mesh.shape["pipe"], mesh.shape["row"], mesh.shape["col"] // 2, FF // (mesh.shape["row"] * BLK))
    return jax.shard_map(functools.partial(local, sizes), mesh=mesh, in_specs=in_specs, out_specs=out_specs, check_vma=False)
```

time: 1060 us -> 195 us (0.18); the launches traced: 1040 us -> 195 us
  waiting for transfers between devices: 514 us -> 0 us
  blocking collectives: 216 us -> 0 us
  Pallas kernels: 0 us -> 188 us
  local copies, waits for them, and re-layouts: 137 us -> 6.55 us
  other arithmetic: 113 us -> 0 us
  matrix products: 39.5 us -> 0 us
  between operations: 15.3 us -> 0.67 us
    reduce_scatter x8 -> x0, waiting for transfers between devices: 425 us -> none  [the longest x5 342 us: local(): lax.psum_scatter(partial_sum, 'row', scatter_dimension=1, tiled=True)]
    pallas_call x0 -> x2, Pallas kernels: none -> 188 us  [the longest x1 182 us: local(): pl.pallas_call(functools.partial(main_kernel, sizes), out_shape=(jax.Shap...]
    all_gather x6 -> x0, blocking collectives: 145 us -> none  [the longest x5 124 us: local(): grad_full = lax.all_gather(incoming, 'row', axis=1, tiled=True)]
    psum x5 -> x0, blocking collectives: 70.6 us -> none  [local(): lax.psum(jnp.sum(local_now * gain_local * own_share, axis=1), 'row')]
    all_gather x4 -> x0, waiting for transfers between devices: 68.4 us -> none  [the longest x1 24.6 us: local(): lax.all_gather(up_weight, 'col', axis=1, tiled=True)]
    another operation x41 -> x0, local copies, waits for them, and re-layouts: 51.3 us -> none
    scatter-add x6 -> x0, other arithmetic: 42.3 us -> none  [spread_blocks(): return jax.ops.segment_sum(product, flat_cols, num_segments=blocks_local)]
    dot_general x13 -> x0, matrix products: 39.5 us -> none  [the longest x6 20.2 us: spread_blocks(): jnp.einsum('trk,rksn->rstn', shaped, blocks, preferred_element_type=jnp.f...]
  transfers between devices with their start and end apart: 16 -> 0, of which waited for: 14 -> 0; matrix products, arithmetic and copies ran while one was open for 11% -> 0% of each run, Pallas kernels for 0% -> 0%
where the time goes in v1:
time: 195 us
  Pallas kernels  188 us (96%)
  local copies, waits for them, and re-layouts  6.55 us (3%)
    pallas_call x1, Pallas kernels, local(): pl.pallas_call(functools.partial(main_kernel, sizes), out_shape=(jax.Shap...  182 us
    pallas_call x1, Pallas kernels, local(): pl.pallas_call(functools.partial(sort_kernel, blocks), out_shape=table +...  5.64 us
    unnamed x16, local copies, waits for them, and re-layouts  5.31 us

profile of v1, /device:TPU:1, one launch (start us, length us, event | category | flops | bytes accessed | tf_op | source)
XLA Modules:
  0.0 195.2 jit_solution(9100693859764833650)
XLA Ops:
  0.6 0.0 copy-start.3
  0.6 0.7 copy-done.3
  1.3 0.1 copy.16
  1.4 0.0 copy-start.4
  1.4 0.6 reshape.36.icol
  2.0 0.1 copy-done.4
  2.1 0.1 copy.17
  2.2 0.6 reshape.38.ocol
  2.8 5.6 %order_slots.1 = (s32[64]{0:T(128)}, f32[64]{0:T(128)}, s32[14]{0:T(128)}, f32[14]{0:T(128)}, s32[64]{0:T(128)}, /*index=5*/f32[64]{0:T(128)}, s32[14]{0:T(128)}, f32[14]{0:T(128)}) custom-call(s32[64]{0:T(128)} %reshape.36.icol, s32[64]{0:T(128)} %reshape.38.ocol), custom_call_target="tpu_custom_call" | custom-call | tf_op jit(solution)/shard_map/order_slots/pallas_call | solution.py:545
  8.4 182.3 %backward.1 = (bf16[2,64,512]{2,1,0:T(8,128)(2,1)}, bf16[512,256]{1,0:T(8,128)(2,1)}, bf16[512,256]{1,0:T(8,128)(2,1)}, bf16[512,256]{1,0:T(8,128)(2,1)}) custom-call(bf16[128,512]{1,0:T(8,128)(2,1)} %bitcast.17, bf16[2,64,512]{2,1,0:T(8,128)(2,1)} %go_ref.1, bf16[1,512]{1,0:T(2,128)(2,1)} %gain_ref.1, bf16[512,256]{1,0:T(8,128)(2,1)} %bitcast.13, ...), custom_call_target="tpu_custom_call" | custom-call | tf_op jit(solution)/shard_map/backward/pallas_call | solution.py:555
  190.8 0.0 copy-start.2
  190.8 1.6 copy.22
  192.4 0.0 copy-done.2
  192.4 0.0 copy-start.1
  192.4 0.7 copy.23
  193.1 0.3 copy-done.1
  193.4 0.0 copy-start
  193.4 0.7 copy.24
  194.1 0.3 copy-done
  194.5 0.7 copy.25
Async XLA Ops:
  0.6 0.7 copy-start.3
  1.4 0.7 copy-start.4
  190.8 1.6 copy-start.2
  192.4 1.0 copy-start.1
  193.4 1.0 copy-start

commit v2 on v0

v2 whole, which is shorter than its diff:
```python
import functools

import jax
import jax.numpy as jnp
from jax import lax
from jax.experimental import pallas as pl
from jax.experimental.pallas import tpu as pltpu
from jax.sharding import PartitionSpec as P

FF = 14336
BLK = 128
EPSILON = 1e-05
MESH = pl.DeviceIdType.MESH
F32 = jnp.float32
BF16 = jnp.bfloat16


CHUNKS = 4
FACTOR_SECTIONS = 2


def dot(a, b):
    return jnp.dot(a, b, preferred_element_type=F32)


def pick(index, values):
    result = values[-1]
    for i in reversed(range(len(values) - 1)):
        result = jnp.where(index == i, values[i], result)
    return result


def slot_table(col):
    block_rows = col.shape[1]
    square = (block_rows, block_rows)
    eye = lax.broadcasted_iota(jnp.int32, square, 0) == lax.broadcasted_iota(jnp.int32, square, 1)
    lane = lax.broadcasted_iota(jnp.int32, (1, block_rows), 1)
    down = lax.broadcasted_iota(jnp.int32, (block_rows, BLK), 0)
    place = lax.broadcasted_iota(jnp.int32, (block_rows, BLK), 1)

    def upright(row):
        return jnp.sum(jnp.where(eye, jnp.broadcast_to(row, square), 0), axis=1, keepdims=True)

    rows = [col[s : s + 1, :] for s in range(2)]
    keys = [rows[s] * (2 * block_rows) + s * block_rows + lane for s in range(2)]
    order, keep, upto, count = 0, 0, 0, 0
    for s in range(2):
        key, block = upright(keys[s]), upright(rows[s])
        rank = sum(jnp.sum(jnp.where(keys[t] < key, 1, 0), axis=1, keepdims=True) for t in range(2))
        first = sum(jnp.sum(jnp.where(rows[t] < block, 1, 0), axis=1, keepdims=True) for t in range(2))
        here = rank == place
        order = order + jnp.sum(jnp.where(here, down + s * block_rows, 0), axis=0, keepdims=True)
        keep = keep + jnp.sum(jnp.where(here, jnp.where(rank != first, 1, 0), 0), axis=0, keepdims=True)
        upto = upto + jnp.sum(jnp.where(block <= place, 1, 0), axis=0, keepdims=True)
        count = count + jnp.sum(jnp.where(block == place, 1, 0), axis=0, keepdims=True)
    return order, keep, jnp.maximum(upto - 1, 0), jnp.minimum(count, 1)


def main_kernel(
    sizes,
    x_ref, go_ref, gain_ref, gate_ref, up_ref, down_ref, icol_rows, ocol_rows,
    icol, icnt, ocol, ocnt,
    gin_ref, ggate_ref, gup_ref, gdown_ref,
    wall, wt, xg, xn, rinv, pg, pu, sg, ab, bb, cb, hb, pool, dhall, dgb, dub, dyg, dyr, xnr, rss, rsr, dgl, dul, hl, acc, tabv, tab,
    tabsem, wsend, wrecv, xsend, xrecv, gsend, grecv, hsend, hrecv, rsend, rrecv,
    asend, arecv, nsend, nrecv, dsend, drecv, csend, crecv, psend, precv, ysend, yrecv,
):
    n_pipe, n_row, n_y, blocks = sizes
    n_col, n_x = 2 * n_y, n_row // 2
    both, width = x_ref.shape
    tokens = both // CHUNKS
    features = width * n_row
    block_rows = features // BLK
    per = block_rows // n_row
    slots = 2 * block_rows
    piece = 3 * BLK
    span = 3 * blocks * both
    block = 2 * per * BLK

    p = lax.axis_index("pipe")
    r = lax.axis_index("row")
    c = lax.axis_index("col")
    y = lax.div(c, 2)
    core = lax.rem(c, 2)
    x = lax.rem(r, n_x)
    by_factors = p <= FACTOR_SECTIONS - 1
    partner = lax.rem(r + n_x, n_row)

    def place(row):
        return lax.rem(row, n_x) * 2 + lax.div(row, n_x)

    def column(dy, dcore):
        return lax.rem(y + dy, n_y) * 2 + lax.rem(core + dcore, 2)

    up_y, down_y, sibling = column(1, 0), column(n_y - 1, 0), column(0, 1)

    barrier = pltpu.get_barrier_semaphore()

    def greet(d, _):
        pl.semaphore_signal(barrier, inc=1, device_id={"row": lax.rem(r + d, n_row)}, device_id_type=MESH)
        pl.semaphore_signal(barrier, inc=1, device_id={"col": lax.rem(c + d, n_col)}, device_id_type=MESH)
        return 0

    lax.fori_loop(1, n_row, greet, 0)

    @pl.when(p > 0)
    def _():
        for row in (r, partner):
            pl.semaphore_signal(barrier, inc=1, device_id={"pipe": p - 1, "row": row}, device_id_type=MESH)

    @pl.when(p < n_pipe - 1)
    def _():
        for row in (r, partner):
            pl.semaphore_signal(barrier, inc=1, device_id={"pipe": p + 1, "row": row}, device_id_type=MESH)

    xg[r, 0:both, :] = x_ref[...]
    xg[r, both : both + 16, :] = jnp.broadcast_to(gain_ref[...].astype(F32), (16, width)).astype(BF16)
    for i in range(per):
        for which, (ref, cnt) in enumerate(((gate_ref, icnt), (up_ref, icnt), (down_ref, ocnt))):
            live = cnt[c * per + i]
            slot = lax.broadcasted_iota(jnp.int32, (BLK, 2 * BLK), 1) // BLK
            value = ref[i * BLK : (i + 1) * BLK, :].astype(F32)
            wall[c, (i * 3 + which) * BLK : (i * 3 + which + 1) * BLK, :] = jnp.where(slot < live, value, 0.0).astype(BF16)

    @pl.when(p == n_pipe - 1)
    def _():
        for k in range(CHUNKS):
            dyg[k, place(r)] = go_ref[k * tokens : (k + 1) * tokens, :]

    pl.semaphore_wait(barrier, n_row - 1 + n_col - 1 + jnp.where(p > 0, 2, 0) + jnp.where(p < n_pipe - 1, 2, 0))

    def remote(src, dst, send, recv, target):
        return pltpu.make_async_remote_copy(src_ref=src, dst_ref=dst, send_sem=send, recv_sem=recv, device_id=target, device_id_type=MESH)

    def weights(owner, q, target, number):
        share = wall.at[owner, pl.ds(pl.multiple_of(q * piece, piece), piece), :]
        return remote(share, share, wsend.at[number], wrecv.at[owner, q], {"col": target})

    def x_copy(owner, target, number):
        return remote(xg.at[owner], xg.at[owner], xsend.at[number], xrecv.at[owner], {"row": target})

    def dy_copy(k, source, target, number):
        pair = dyg.at[k, pl.ds(source * 2, 2)]
        row = lax.div(r, n_x) * n_x + target
        return remote(pair, pair, gsend.at[k, number], grecv.at[k, source], {"row": row})

    def hop_copy(k, pipe, row, number):
        rows = pl.ds(pl.multiple_of(k * tokens, tokens), tokens)
        return remote(gin_ref.at[rows, :], dyg.at[k, place(r)], hsend.at[k, number], hrecv.at[k, number], {"pipe": pipe, "row": row})

    def swap_copy(k):
        share = dyg.at[k, place(r)]
        return remote(share, share, hsend.at[k, 1], hrecv.at[k, 1], {"row": partner})

    def sum_copy(k, target, source, number):
        return remote(rss.at[k, target], rsr.at[k, source], rsend.at[k, number], rrecv.at[k, source], {"row": target})

    def factor_copy(owner, target, number):
        share = pool.at[pl.ds(pl.multiple_of(owner * span, span), span), :]
        return remote(share, share, asend.at[number], arecv.at[owner], {"col": target})

    def share_start(part, which, k):
        if part < 2:
            return ((part * 3 + which) * n_y + k) * block
        return (6 * n_y + ((part - 2) * 3 + which) * (n_y - 1) + k - 1) * block

    def shares(part, which, k):
        return pl.ds(pl.multiple_of(share_start(part, which, k), block), block)

    def pair_copy(which, k):
        return remote(pool.at[shares(0, which, k), :], pool.at[shares(1, which, k), :], psend.at[which, k], precv.at[which, k], {"col": sibling})

    def ring_copy(which, k, target):
        return remote(pool.at[shares(2, which, k), :], pool.at[shares(3, which, k), :], ysend.at[which, k], yrecv.at[which, k], {"col": target})

    def dh_copy(k, owner, target, number):
        return remote(dhall.at[k, owner], dhall.at[k, owner], dsend.at[k, number], drecv.at[k, owner], {"col": target})

    def xn_copy(target, source, number):
        return remote(xn.at[pl.ds(target * per, per)], xnr.at[source], nsend.at[number], nrecv.at[source], {"col": target})

    def dyc_copy(k, target, source, number):
        return remote(dyg.at[k, place(target)], dyr.at[k, source], csend.at[k, number], crecv.at[k, source], {"col": target})

    def send_dy(k):
        def body(d, _):
            dy_copy(k, x, lax.rem(x + d, n_x), d).start()
            return 0

        lax.fori_loop(1, n_x, body, 0)

    def send_x(d, _):
        x_copy(r, lax.rem(r + d, n_row), d).start()
        return 0

    for q in range(per):
        weights(c, q, up_y, q).start()
        weights(c, (q + 2) % per, down_y, per + q).start()
    lax.fori_loop(1, n_row, send_x, 0)
    for q in range(per):
        weights(c, q, sibling, 8 + q).start()

    @pl.when(p == n_pipe - 1)
    def _():
        def body(k, _):
            swap_copy(k).start()
            return 0

        lax.fori_loop(0, CHUNKS, body, 0)

    for at, ref in ((0, icol_rows), (4, ocol_rows)):
        for row, value in enumerate(slot_table(ref[...])):
            tabv[at + row : at + row + 1, :] = value
    table = pltpu.make_async_copy(tabv, tab, tabsem)
    table.start()
    acc[...] = jnp.zeros_like(acc)
    table.wait()

    rinv[...] = jnp.zeros_like(rinv)

    def squares(d, _):
        owner = lax.rem(r + d, n_row)

        @pl.when(d > 0)
        def _():
            x_copy(owner, owner, 0).wait_recv()

        total = rinv[...]
        for i in range(per):
            value = xg[owner, 0:both, i * BLK : (i + 1) * BLK].astype(F32)
            total = total + value * value
        rinv[...] = total
        return 0

    lax.fori_loop(0, n_row, squares, 0)
    mean = jnp.sum(rinv[...], axis=1, keepdims=True) / features
    rinv[...] = jnp.broadcast_to(lax.rsqrt(mean + EPSILON), (both, BLK))

    def norm(owner, _):
        scale = rinv[...]
        for i in range(per):
            lanes = slice(i * BLK, (i + 1) * BLK)
            gain = xg[owner, both : both + 16, lanes].astype(F32)[0:1, :]
            value = xg[owner, 0:both, lanes].astype(F32)
            xn[owner * per + i] = (value * scale * gain).astype(BF16)
        return 0

    lax.fori_loop(0, n_row, norm, 0)

    def first_dy(k, _):
        swap_copy(k).wait_recv()
        send_dy(k)
        return 0

    @pl.when(p == n_pipe - 1)
    def _():
        lax.fori_loop(0, CHUNKS, first_dy, 0)

    def use(owner, q):
        block_row = owner * per + q
        value = xn[block_row]
        for which, out in ((0, pg), (1, pu)):
            rows = pl.ds(pl.multiple_of(q * piece + which * BLK, BLK), BLK)
            weight = wall[owner, rows, :]
            product = dot(value, weight)
            out[block_row] = product[:, :BLK]
            out[block_rows + block_row] = product[:, BLK:]
            wt[block_row, which * 2 * BLK : (which + 1) * 2 * BLK, :] = weight.T

    turns = (0, 0, 0, 0, n_y - 1, 1, n_y - 1, 1, n_y - 1, 1, n_y - 1, 1, 2, 2, 2, 2)
    quarters = (0, 1, 2, 3, 0, 2, 1, 3, 2, 0, 3, 1, 0, 2, 1, 3)
    steps = len(turns)

    def arrive(s, _):
        @pl.when(s < steps)
        def _():
            q = pick(s, quarters)
            owner = column(pick(s, turns), 0)

            @pl.when(s >= 4)
            def _():
                weights(owner, q, sibling, 0).wait_recv()

                @pl.when(s < 8)
                def _():
                    target = jnp.where(lax.rem(s, 2) == 0, up_y, down_y)
                    weights(owner, q, target, 8 + s).start()

                weights(owner, q, sibling, 12 + s).start()

            use(owner, q)

        @pl.when(s >= 2)
        def _():
            q = pick(s - 2, quarters)
            owner = column(pick(s - 2, turns), 1)
            weights(owner, q, sibling, 0).wait_recv()
            use(owner, q)

        return 0

    lax.fori_loop(0, steps + 2, arrive, 0)

    def add_slots(at, source, rows):
        def body(i, total):
            total = total * tab[at + 1, i].astype(F32) + source[tab[at, i], 0:rows, :]
            sg[i, 0:rows, :] = total
            return total

        lax.fori_loop(0, slots, body, jnp.zeros((rows, BLK), F32), unroll=4)

    add_slots(0, pg, both)

    def gates(j, _):
        ab[j] = sg[tab[2, j]] * tab[3, j].astype(F32)
        return 0

    lax.fori_loop(0, blocks, gates, 0)
    add_slots(0, pu, both)

    def hidden(j, _):
        g = ab[j]
        u = sg[tab[2, j]] * tab[3, j].astype(F32)
        s = jax.nn.sigmoid(g)
        a = u * s * (1.0 + g * (1.0 - s))
        b = g * s
        ab[j] = a
        bb[j] = b
        cb[j] = a * g + b * u
        h = (b * u).astype(BF16)
        hb[j] = h

        @pl.when(by_factors)
        def _():
            for which, value in enumerate((a.astype(BF16), b.astype(BF16), h)):
                pool[pl.ds(pl.multiple_of(c * span + (which * blocks + j) * both, both), both), :] = value

        return 0

    lax.fori_loop(0, blocks, hidden, 0)

    def send_xn(d, _):
        xn_copy(lax.rem(c + d, n_col), c, d).start()
        return 0

    def send_factors():
        for d in range(1, n_y):
            factor_copy(c, column(d, 0), d - 1).start()
        factor_copy(c, sibling, n_y - 1).start()

    def products(k):
        def body(d, _):
            from_x = lax.rem(x + d, n_x)

            @pl.when(d > 0)
            def _():
                dy_copy(k, from_x, from_x, 0).wait_recv()

            for z in range(2):
                owner = z * n_x + from_x
                for i in range(per):
                    block_row = owner * per + i
                    product = dot(dyg[k, from_x * 2 + z, :, i * BLK : (i + 1) * BLK], wall[owner, (i * 3 + 2) * BLK : (i * 3 + 3) * BLK, :])
                    pg[block_row, 0:tokens, :] = product[:, :BLK]
                    pg[block_rows + block_row, 0:tokens, :] = product[:, BLK:]
            return 0

        lax.fori_loop(0, n_x, body, 0)

    def back(k):
        mine = pl.ds(pl.multiple_of(k * tokens, tokens), tokens)
        add_slots(4, pg, tokens)

        def gated(j, total):
            dh = sg[tab[6, j], 0:tokens, :] * tab[7, j].astype(F32)
            dgb[j, mine, :] = (dh * ab[j, mine, :]).astype(BF16)
            dub[j, mine, :] = (dh * bb[j, mine, :]).astype(BF16)
            dhall[k, c, j] = dh.astype(BF16)
            return total + dh * cb[j, mine, :]

        total = lax.fori_loop(0, blocks, gated, jnp.zeros((tokens, BLK), F32))

        @pl.when(by_factors)
        def _():
            for d in range(1, n_y):
                dh_copy(k, c, column(d, 0), d - 1).start()
            dh_copy(k, c, sibling, n_y - 1).start()

        stat = jnp.sum(total, axis=1, keepdims=True)
        high = stat.astype(BF16).astype(F32)
        lane = lax.broadcasted_iota(jnp.int32, (tokens, BLK), 1)
        stat = jnp.where(lane < BLK // 2, high, stat - high).astype(BF16)

        def body(d, _):
            owner = lax.rem(r + d, n_row)
            for i in range(per):
                block_row = owner * per + i
                j0, j1 = icol[0, block_row], icol[1, block_row]
                left = jnp.concatenate([dgb[j0, mine, :], dgb[j1, mine, :], dub[j0, mine, :], dub[j1, mine, :]], axis=1)
                rss[k, owner, :, i * BLK : (i + 1) * BLK] = dot(left, wt[block_row]).astype(BF16)
            rss[k, owner, :, width : width + BLK] = stat

            @pl.when(d < n_row)
            def _():
                sum_copy(k, owner, r, d).start()

            return 0

        lax.fori_loop(1, n_row + 1, body, 0)

        @pl.when(by_factors)
        def _():
            dyr[k, c] = dyg[k, place(c)]

            def send(d, _):
                dyc_copy(k, lax.rem(c + d, n_col), c, d).start()
                return 0

            lax.fori_loop(1, n_col, send, 0)

    def finish(k):
        mine = pl.ds(pl.multiple_of(k * tokens, tokens), tokens)

        def body(d, total):
            owner = lax.rem(r + d, n_row)
            sum_copy(k, owner, owner, 0).wait_recv()
            return total + rsr[k, owner].astype(F32)

        total = lax.fori_loop(1, n_row, body, rss[k, r].astype(F32))
        stat = jnp.sum(total[:, width:], axis=1, keepdims=True) / (BLK // 2)
        scale = rinv[mine, :][:, 0:1]
        gain = xg[r, both : both + 16, :].astype(F32)[0:1, :]
        value = xg[r, mine, :].astype(F32)
        result = dyg[k, place(r)].astype(F32) + gain * scale * total[:, :width]
        result = result - value * (scale * scale * stat / features)
        gin_ref[mine, :] = result.astype(BF16)

        @pl.when(p > 0)
        def _():
            hop_copy(k, p - 1, r, 0).start()
            hop_copy(k, p - 1, partner, 1).start()

    def take_dy(k):
        @pl.when(p < n_pipe - 1)
        def _():
            hop_copy(k, p + 1, r, 0).wait_recv()
            hop_copy(k, p + 1, partner, 1).wait_recv()
            send_dy(k)

    def pass_on(k):
        for d in range(1, n_y):
            owner = column(d, 0)

            @pl.when(k == 0)
            def _(owner=owner, d=d):
                factor_copy(owner, owner, 0).wait_recv()
                factor_copy(owner, sibling, n_y - 1 + d).start()

            dh_copy(k, owner, owner, 0).wait_recv()
            dh_copy(k, owner, sibling, n_y - 1 + d).start()

    def down_part(k):
        @pl.when(k == 0)
        def _():
            def body(d, _):
                other = lax.rem(c + d, n_col)
                xn_copy(other, other, 0).wait_recv()
                return 0

            lax.fori_loop(1, n_col, body, 0)

        def body(d, _):
            other = lax.rem(c + d, n_col)
            dyc_copy(k, other, other, 0).wait_recv()
            return 0

        lax.fori_loop(1, n_col, body, 0)

    def grads(k):
        mine = pl.ds(pl.multiple_of(k * tokens, tokens), tokens)
        for d in range(n_y):
            owner = column(d, 1)

            @pl.when(k == 0)
            def _(owner=owner):
                factor_copy(owner, sibling, 0).wait_recv()

            dh_copy(k, owner, sibling, 0).wait_recv()

        def body(j, _):
            for o in range(n_col):
                rows = slice(o * tokens, (o + 1) * tokens)
                dh = dhall[k, o, j].astype(F32)
                a, b, h = (
                    pool[pl.ds(pl.multiple_of(o * span + (which * blocks + j) * both + k * tokens, tokens), tokens), :] for which in range(3)
                )
                dgl[j, rows, :] = (dh * a.astype(F32)).astype(BF16)
                dul[j, rows, :] = (dh * b.astype(F32)).astype(BF16)
                hl[j, rows, :] = h
            return 0

        lax.fori_loop(0, blocks, body, 0)
        for i in range(per):
            block_row = c * per + i
            j0, j1 = icol[0, block_row], icol[1, block_row]
            q0, q1 = ocol[0, block_row], ocol[1, block_row]
            left = jnp.concatenate([xnr[o, i, mine, :] for o in range(n_col)], axis=0).T
            acc[0, i] = acc[0, i] + dot(left, jnp.concatenate([dgl[j0], dgl[j1]], axis=1))
            acc[1, i] = acc[1, i] + dot(left, jnp.concatenate([dul[j0], dul[j1]], axis=1))
            left = jnp.concatenate([dyr[k, o, :, i * BLK : (i + 1) * BLK] for o in range(n_col)], axis=0).T
            acc[2, i] = acc[2, i] + dot(left, jnp.concatenate([hl[q0], hl[q1]], axis=1))

    def own_grads(owner, emit):
        for i in range(per):
            block_row = owner * per + i
            j0, j1 = icol[0, block_row], icol[1, block_row]
            q0, q1 = ocol[0, block_row], ocol[1, block_row]
            left = xn[block_row].T
            emit(0, i, dot(left, jnp.concatenate([dgb[j0], dgb[j1]], axis=1)))
            emit(1, i, dot(left, jnp.concatenate([dub[j0], dub[j1]], axis=1)))
            dy = jnp.concatenate([dyg[k, place(owner), :, i * BLK : (i + 1) * BLK] for k in range(CHUNKS)], axis=0)
            emit(2, i, dot(dy.T, jnp.concatenate([hb[q0], hb[q1]], axis=1)))

    def part_rows(part, which, k, i, s):
        start = share_start(part, which, k) + (i * 2 + s) * BLK
        return pl.ds(pl.multiple_of(start, BLK), BLK)

    def put(part, which, k, i, value):
        for s in range(2):
            pool[part_rows(part, which, k, i, s), :] = value[:, s * BLK : (s + 1) * BLK].astype(BF16)

    def get(part, which, k, i):
        return jnp.concatenate([pool[part_rows(part, which, k, i, s), :] for s in range(2)], axis=1).astype(F32)

    def to_sibling(k, _):
        own_grads(lax.rem(y + k, n_y) * 2 + (1 - core), lambda which, i, value: put(0, which, k, i, value))
        for which in range(3):
            pair_copy(which, k).start()
        return 0

    def to_ring(step, _):
        k = pick(step, (2, 1, 3, 0))
        target = lax.rem(y + k, n_y) * 2 + core
        for which in range(3):
            pair_copy(which, k).wait_recv()

        def emit(which, i, value):
            value = value + get(1, which, k, i)
            acc[which, i] = value

            @pl.when(k > 0)
            def _():
                put(2, which, k, i, value)

        own_grads(target, emit)

        @pl.when(k > 0)
        def _():
            for which in range(3):
                ring_copy(which, k, target).start()

        return 0

    def collect(k, _):
        for which in range(3):
            ring_copy(which, k, sibling).wait_recv()
            for i in range(per):
                acc[which, i] = acc[which, i] + get(3, which, k, i)
        return 0

    @pl.when(by_factors)
    def _():
        xnr[c] = xn[pl.ds(c * per, per)]
        send_factors()
        lax.fori_loop(1, n_col, send_xn, 0)

    take_dy(0)

    def step(s, _):
        @pl.when(s < CHUNKS)
        def _():
            products(s)

            @pl.when(s < CHUNKS - 1)
            def _():
                take_dy(s + 1)

            back(s)

        @pl.when(jnp.logical_and(s >= lead + 1, s < lead + 1 + CHUNKS))
        def _():
            grads(s - lead - 1)

        @pl.when(jnp.logical_and(s >= lead, s < lead + CHUNKS))
        def _():
            down_part(s - lead)
            pass_on(s - lead)

        @pl.when(jnp.logical_and(s >= 1, s < CHUNKS + 1))
        def _():
            finish(s - 1)

        return 0

    lead = jnp.where(p == 0, 1, jnp.where(by_factors, CHUNKS + 1, 3 * CHUNKS))
    lax.fori_loop(0, 2 * CHUNKS + 2, step, 0)

    @pl.when(jnp.logical_not(by_factors))
    def _():
        lax.fori_loop(0, n_y, to_sibling, 0)
        lax.fori_loop(0, n_y, to_ring, 0)
        lax.fori_loop(1, n_y, collect, 0)

    for i in range(per):
        for which, (ref, cnt) in enumerate(((ggate_ref, icnt), (gup_ref, icnt), (gdown_ref, ocnt))):
            live = cnt[c * per + i]
            slot = lax.broadcasted_iota(jnp.int32, (BLK, 2 * BLK), 1) // BLK
            ref[i * BLK : (i + 1) * BLK, :] = jnp.where(slot < live, acc[which, i], 0.0).astype(BF16)

    def sent_weights(number, _):
        weights(c, 0, sibling, number).wait_send()
        return 0

    lax.fori_loop(0, 28, sent_weights, 0)

    def sent(d, _):
        other = lax.rem(r + d, n_row)
        x_copy(r, other, d).wait_send()
        for k in range(CHUNKS):
            sum_copy(k, other, r, d).wait_send()
        return 0

    lax.fori_loop(1, n_row, sent, 0)

    def sent_dy(d, _):
        for k in range(CHUNKS):
            dy_copy(k, x, lax.rem(x + d, n_x), d).wait_send()
        return 0

    lax.fori_loop(1, n_x, sent_dy, 0)

    @pl.when(p == n_pipe - 1)
    def _():
        for k in range(CHUNKS):
            swap_copy(k).wait_send()

    @pl.when(p > 0)
    def _():
        for k in range(CHUNKS):
            hop_copy(k, p - 1, r, 0).wait_send()
            hop_copy(k, p - 1, partner, 1).wait_send()

    @pl.when(jnp.logical_not(by_factors))
    def _():
        for which in range(3):
            for k in range(n_y):
                pair_copy(which, k).wait_send()
                if k > 0:
                    ring_copy(which, k, sibling).wait_send()

    @pl.when(by_factors)
    def _():
        def sent_beside(d, _):
            beside = lax.rem(c + d, n_col)
            xn_copy(beside, c, d).wait_send()
            for k in range(CHUNKS):
                dyc_copy(k, beside, c, d).wait_send()
            return 0

        lax.fori_loop(1, n_col, sent_beside, 0)

        def sent_factors(number, _):
            factor_copy(c, sibling, number).wait_send()
            for k in range(CHUNKS):
                dh_copy(k, c, sibling, number).wait_send()
            return 0

        lax.fori_loop(0, 2 * n_y - 1, sent_factors, 0)


def hand_over(a, b, c, d, out_a, out_b, out_c, out_d):
    for src, dst in ((a, out_a), (b, out_b), (c, out_c), (d, out_d)):
        dst[...] = src[...]


def local(sizes, inputs, grad_out, norm_gain, gate_weight, up_weight, down_weight, inner_cols, inner_counts, outer_cols, outer_counts):
    n_pipe, n_row, n_y, blocks = sizes
    n_col, n_x = 2 * n_y, n_row // 2
    _, micro, tokens, width = inputs.shape
    both = micro * tokens
    small = both // CHUNKS
    block_rows = width * n_row // BLK
    per = block_rows // n_row
    slots = 2 * block_rows
    rows = gate_weight.shape[1]
    icol, ocol = inner_cols[0].T, outer_cols[0].T
    icnt, ocnt = inner_counts.reshape(block_rows), outer_counts.reshape(block_rows)
    smem = pl.BlockSpec(memory_space=pltpu.SMEM)
    vmem = pl.BlockSpec(memory_space=pltpu.VMEM)
    dma = pltpu.SemaphoreType.DMA
    weight_out = jax.ShapeDtypeStruct((rows, 2 * BLK), BF16)
    outs = (jax.ShapeDtypeStruct((both, width), BF16), weight_out, weight_out, weight_out)
    results = pl.pallas_call(
        functools.partial(main_kernel, sizes),
        out_shape=outs,
        in_specs=[vmem] * 8 + [smem] * 4,
        out_specs=[vmem] * 4,
        scratch_shapes=[
            pltpu.VMEM((n_col, 3 * rows, 2 * BLK), BF16),
            pltpu.VMEM((block_rows, 4 * BLK, BLK), BF16),
            pltpu.VMEM((n_row, both + 16, width), BF16),
            pltpu.VMEM((block_rows, both, BLK), BF16),
            pltpu.VMEM((both, BLK), F32),
            pltpu.VMEM((slots, both, BLK), F32),
            pltpu.VMEM((slots, both, BLK), F32),
            pltpu.VMEM((slots, both, BLK), F32),
            pltpu.VMEM((blocks, both, BLK), F32),
            pltpu.VMEM((blocks, both, BLK), F32),
            pltpu.VMEM((blocks, both, BLK), F32),
            pltpu.VMEM((blocks, both, BLK), BF16),
            pltpu.VMEM((max(n_col * 3 * blocks * both, (12 * n_y - 6) * 2 * rows), BLK), BF16),
            pltpu.VMEM((CHUNKS, n_col, blocks, small, BLK), BF16),
            pltpu.VMEM((blocks, both, BLK), BF16),
            pltpu.VMEM((blocks, both, BLK), BF16),
            pltpu.VMEM((CHUNKS, n_row, small, width), BF16),
            pltpu.VMEM((CHUNKS, n_col, small, width), BF16),
            pltpu.VMEM((n_col, per, both, BLK), BF16),
            pltpu.VMEM((CHUNKS, n_row, small, width + BLK), BF16),
            pltpu.VMEM((CHUNKS, n_row, small, width + BLK), BF16),
            pltpu.VMEM((blocks, n_col * small, BLK), BF16),
            pltpu.VMEM((blocks, n_col * small, BLK), BF16),
            pltpu.VMEM((blocks, n_col * small, BLK), BF16),
            pltpu.VMEM((3, per, BLK, 2 * BLK), F32),
            pltpu.VMEM((8, BLK), jnp.int32),
            pltpu.SMEM((8, BLK), jnp.int32),
            dma,
            dma((28,)), dma((n_col, per)),
            dma((n_row,)), dma((n_row,)),
            dma((CHUNKS, n_x)), dma((CHUNKS, n_x)),
            dma((CHUNKS, 2)), dma((CHUNKS, 2)),
            dma((CHUNKS, n_row)), dma((CHUNKS, n_row)),
            dma((2 * n_y - 1,)), dma((n_col,)),
            dma((n_col,)), dma((n_col,)),
            dma((CHUNKS, 2 * n_y - 1)), dma((CHUNKS, n_col)),
            dma((CHUNKS, n_col)), dma((CHUNKS, n_col)),
            dma((3, n_y)), dma((3, n_y)),
            dma((3, n_y)), dma((3, n_y)),
        ],
        compiler_params=pltpu.CompilerParams(collective_id=0, has_side_effects=True, vmem_limit_bytes=60 * 1024 * 1024),
        name="backward",
    )(
        inputs.reshape(both, width), grad_out.reshape(both, width), norm_gain,
        gate_weight.reshape(rows, 2 * BLK), up_weight.reshape(rows, 2 * BLK), down_weight.reshape(rows, 2 * BLK),
        icol, ocol, icol, icnt, ocol, ocnt,
    )
    grad_in, gate, up, down = pl.pallas_call(
        hand_over,
        out_shape=outs,
        in_specs=[vmem] * 4,
        out_specs=[vmem] * 4,
        name="hand_over",
    )(*results)
    return grad_in.reshape(inputs.shape), gate[None], up[None], down[None]


def solution(mesh):
    in_specs = (
        P("pipe", None, "col", "row"),
        P(None, "col", "row"),
        P("pipe", "row"),
        P("pipe", "col", "row"),
        P("pipe", "col", "row"),
        P("pipe", "col", "row"),
        P("pipe", None, "row"),
        P("pipe", None, "row"),
        P("pipe", None, "row"),
        P("pipe", None, "row"),
    )
    out_specs = (
        P("pipe", None, "col", "row"),
        P("pipe", "col", "row"),
        P("pipe", "col", "row"),
        P("pipe", "col", "row"),
    )
    sizes = (mesh.shape["pipe"], mesh.shape["row"], mesh.shape["col"] // 2, FF // (mesh.shape["row"] * BLK))
    return jax.shard_map(functools.partial(local, sizes), mesh=mesh, in_specs=in_specs, out_specs=out_specs, check_vma=False)
```

time: 1060 us -> 156 us (0.15); the launches traced: 1040 us -> 155 us
  waiting for transfers between devices: 514 us -> 0 us
  blocking collectives: 216 us -> 0 us
  Pallas kernels: 0 us -> 155 us
  local copies, waits for them, and re-layouts: 137 us -> 0 us
  other arithmetic: 113 us -> 0 us
  matrix products: 39.5 us -> 0 us
  between operations: 15.3 us -> 0.64 us
    reduce_scatter x8 -> x0, waiting for transfers between devices: 425 us -> none  [the longest x5 342 us: local(): lax.psum_scatter(partial_sum, 'row', scatter_dimension=1, tiled=True)]
    pallas_call x0 -> x2, Pallas kernels: none -> 155 us  [the longest x1 153 us: local(): pl.pallas_call(functools.partial(main_kernel, sizes), out_shape=outs, in_...]
    all_gather x6 -> x0, blocking collectives: 145 us -> none  [the longest x5 124 us: local(): grad_full = lax.all_gather(incoming, 'row', axis=1, tiled=True)]
    psum x5 -> x0, blocking collectives: 70.6 us -> none  [local(): lax.psum(jnp.sum(local_now * gain_local * own_share, axis=1), 'row')]
    all_gather x4 -> x0, waiting for transfers between devices: 68.4 us -> none  [the longest x1 24.6 us: local(): lax.all_gather(up_weight, 'col', axis=1, tiled=True)]
    another operation x41 -> x0, local copies, waits for them, and re-layouts: 51.3 us -> none
    scatter-add x6 -> x0, other arithmetic: 42.3 us -> none  [spread_blocks(): return jax.ops.segment_sum(product, flat_cols, num_segments=blocks_local)]
    dot_general x13 -> x0, matrix products: 39.5 us -> none  [the longest x6 20.2 us: spread_blocks(): jnp.einsum('trk,rksn->rstn', shaped, blocks, preferred_element_type=jnp.f...]
  transfers between devices with their start and end apart: 16 -> 0, of which waited for: 14 -> 0; matrix products, arithmetic and copies ran while one was open for 11% -> 0% of each run, Pallas kernels for 0% -> 0%
where the time goes in v2:
time: 156 us; the launch traced here: 155 us
  Pallas kernels  155 us (99%)
    pallas_call x1, Pallas kernels, local(): pl.pallas_call(functools.partial(main_kernel, sizes), out_shape=outs, in_...  153 us

profile of v2, /device:TPU:1, one launch (start us, length us, event | category | flops | bytes accessed | tf_op | source)
XLA Modules:
  0.0 155.4 jit_solution(4858444745059200658)
XLA Ops:
  0.6 152.7 %backward.1 = (bf16[128,512]{1,0:T(8,128)(2,1)}, bf16[512,256]{1,0:T(8,128)(2,1)}, bf16[512,256]{1,0:T(8,128)(2,1)}, bf16[512,256]{1,0:T(8,128)(2,1)}) custom-call(bf16[128,512]{1,0:T(8,128)(2,1)} %bitcast.20, bf16[128,512]{1,0:T(8,128)(2,1)} %bitcast.21, bf16[1,512]{1,0:T(2,128)(2,1)} %gain_ref.1, bf16[512,256]{1,0:T(8,128)(2,1)} %bitcast.17, ...), custom_call_target="tpu_custom_call" | custom-call | tf_op jit(solution)/shard_map/backward/pallas_call | solution.py:703
  153.3 2.1 %hand_over.1 = (bf16[128,512]{1,0:T(8,128)(2,1)}, bf16[512,256]{1,0:T(8,128)(2,1)}, bf16[512,256]{1,0:T(8,128)(2,1)}, bf16[512,256]{1,0:T(8,128)(2,1)}) custom-call(bf16[128,512]{1,0:T(8,128)(2,1)} %get-tuple-element.12.a, bf16[512,256]{1,0:T(8,128)(2,1)} %get-tuple-element.13.b, bf16[512,256]{1,0:T(8,128)(2,1)} %get-tuple-element.14.c, ...), custom_call_target="tpu_custom_call" | custom-call | tf_op jit(solution)/shard_map/hand_over/pallas_call | solution.py:756

commit v3 on v2

--- a/solution.py
+++ b/solution.py
@@ -15,8 +15,11 @@
 BF16 = jnp.bfloat16
 
 
-CHUNKS = 4
+CHUNKS = 8
 FACTOR_SECTIONS = 2
+AHEAD = 1
+LATE = 1
+FACTORS_LATE = 2
 
 
 def dot(a, b):
@@ -61,7 +64,7 @@
     x_ref, go_ref, gain_ref, gate_ref, up_ref, down_ref, icol_rows, ocol_rows,
     icol, icnt, ocol, ocnt,
     gin_ref, ggate_ref, gup_ref, gdown_ref,
-    wall, wt, xg, xn, rinv, pg, pu, sg, ab, bb, cb, hb, pool, dhall, dgb, dub, dyg, dyr, xnr, rss, rsr, dgl, dul, hl, acc, tabv, tab,
+    wall, wt, xg, xn, rinv, pg, pu, sg, ab, bb, cb, hb, pool, dhall, dgb, dub, dyg, dyr, xnr, rss, rsr, al, bl, hl, dgl, dul, xnt, acc, tabv, tab,
     tabsem, wsend, wrecv, xsend, xrecv, gsend, grecv, hsend, hrecv, rsend, rrecv,
     asend, arecv, nsend, nrecv, dsend, drecv, csend, crecv, psend, precv, ysend, yrecv,
 ):
@@ -74,7 +77,7 @@
     per = block_rows // n_row
     slots = 2 * block_rows
     piece = 3 * BLK
-    span = 3 * blocks * both
+    span = 2 * blocks * both
     block = 2 * per * BLK
 
     p = lax.axis_index("pipe")
@@ -307,7 +310,7 @@
             sg[i, 0:rows, :] = total
             return total
 
-        lax.fori_loop(0, slots, body, jnp.zeros((rows, BLK), F32), unroll=4)
+        lax.fori_loop(0, slots, body, jnp.zeros((rows, BLK), F32), unroll=4 if rows > 64 else 16)
 
     add_slots(0, pg, both)
 
@@ -332,7 +335,7 @@
 
         @pl.when(by_factors)
         def _():
-            for which, value in enumerate((a.astype(BF16), b.astype(BF16), h)):
+            for which, value in enumerate((g.astype(BF16), u.astype(BF16))):
                 pool[pl.ds(pl.multiple_of(c * span + (which * blocks + j) * both, both), both), :] = value
 
         return 0
@@ -378,7 +381,7 @@
             dhall[k, c, j] = dh.astype(BF16)
             return total + dh * cb[j, mine, :]
 
-        total = lax.fori_loop(0, blocks, gated, jnp.zeros((tokens, BLK), F32))
+        total = lax.fori_loop(0, blocks, gated, jnp.zeros((tokens, BLK), F32), unroll=2)
 
         @pl.when(by_factors)
         def _():
@@ -391,22 +394,19 @@
         lane = lax.broadcasted_iota(jnp.int32, (tokens, BLK), 1)
         stat = jnp.where(lane < BLK // 2, high, stat - high).astype(BF16)
 
-        def body(d, _):
-            owner = lax.rem(r + d, n_row)
-            for i in range(per):
-                block_row = owner * per + i
-                j0, j1 = icol[0, block_row], icol[1, block_row]
-                left = jnp.concatenate([dgb[j0, mine, :], dgb[j1, mine, :], dub[j0, mine, :], dub[j1, mine, :]], axis=1)
-                rss[k, owner, :, i * BLK : (i + 1) * BLK] = dot(left, wt[block_row]).astype(BF16)
-            rss[k, owner, :, width : width + BLK] = stat
-
-            @pl.when(d < n_row)
-            def _():
-                sum_copy(k, owner, r, d).start()
-
-            return 0
-
-        lax.fori_loop(1, n_row + 1, body, 0)
+        turns = [(1, 2), (1, 1), (1, 3), (0, 2), (1, 0), (0, 1), (0, 3), (0, 0)]
+        for group in (turns[:4], turns[4:]):
+            owners = [lax.rem(lax.div(r, n_x) + dz, 2) * n_x + lax.rem(x + dx, n_x) for dz, dx in group]
+            for owner in owners:
+                for i in range(per):
+                    block_row = owner * per + i
+                    j0, j1 = icol[0, block_row], icol[1, block_row]
+                    left = jnp.concatenate([dgb[j0, mine, :], dgb[j1, mine, :], dub[j0, mine, :], dub[j1, mine, :]], axis=1)
+                    rss[k, owner, :, i * BLK : (i + 1) * BLK] = dot(left, wt[block_row]).astype(BF16)
+                rss[k, owner, :, width : width + BLK] = stat
+            for (dz, dx), owner in zip(group, owners):
+                if dz or dx:
+                    sum_copy(k, owner, r, dz * n_x + dx).start()
 
         @pl.when(by_factors)
         def _():
@@ -421,12 +421,11 @@
     def finish(k):
         mine = pl.ds(pl.multiple_of(k * tokens, tokens), tokens)
 
-        def body(d, total):
+        total = rss[k, r].astype(F32)
+        for d in range(1, n_row):
             owner = lax.rem(r + d, n_row)
             sum_copy(k, owner, owner, 0).wait_recv()
-            return total + rsr[k, owner].astype(F32)
-
-        total = lax.fori_loop(1, n_row, body, rss[k, r].astype(F32))
+            total = total + rsr[k, owner].astype(F32)
         stat = jnp.sum(total[:, width:], axis=1, keepdims=True) / (BLK // 2)
         scale = rinv[mine, :][:, 0:1]
         gain = xg[r, both : both + 16, :].astype(F32)[0:1, :]
@@ -447,19 +446,21 @@
             hop_copy(k, p + 1, partner, 1).wait_recv()
             send_dy(k)
 
+    def spread_factors():
+        for d in range(1, n_y):
+            owner = column(d, 0)
+            factor_copy(owner, owner, 0).wait_recv()
+            factor_copy(owner, sibling, n_y - 1 + d).start()
+
     def pass_on(k):
         for d in range(1, n_y):
             owner = column(d, 0)
-
-            @pl.when(k == 0)
-            def _(owner=owner, d=d):
-                factor_copy(owner, owner, 0).wait_recv()
-                factor_copy(owner, sibling, n_y - 1 + d).start()
-
             dh_copy(k, owner, owner, 0).wait_recv()
             dh_copy(k, owner, sibling, n_y - 1 + d).start()
 
-    def down_part(k):
+    def prepare(k):
+        mine = pl.ds(pl.multiple_of(k * tokens, tokens), tokens)
+
         @pl.when(k == 0)
         def _():
             def body(d, _):
@@ -468,47 +469,52 @@
                 return 0
 
             lax.fori_loop(1, n_col, body, 0)
-
-        def body(d, _):
+            for d in range(n_y):
+                factor_copy(column(d, 1), sibling, 0).wait_recv()
+
+        def arrive(d, _):
             other = lax.rem(c + d, n_col)
             dyc_copy(k, other, other, 0).wait_recv()
             return 0
 
-        lax.fori_loop(1, n_col, body, 0)
-
-    def grads(k):
-        mine = pl.ds(pl.multiple_of(k * tokens, tokens), tokens)
-        for d in range(n_y):
-            owner = column(d, 1)
-
-            @pl.when(k == 0)
-            def _(owner=owner):
-                factor_copy(owner, sibling, 0).wait_recv()
-
-            dh_copy(k, owner, sibling, 0).wait_recv()
+        lax.fori_loop(1, n_col, arrive, 0)
 
         def body(j, _):
             for o in range(n_col):
                 rows = slice(o * tokens, (o + 1) * tokens)
-                dh = dhall[k, o, j].astype(F32)
-                a, b, h = (
-                    pool[pl.ds(pl.multiple_of(o * span + (which * blocks + j) * both + k * tokens, tokens), tokens), :] for which in range(3)
+                g, u = (
+                    pool[pl.ds(pl.multiple_of(o * span + (which * blocks + j) * both + k * tokens, tokens), tokens), :].astype(F32)
+                    for which in range(2)
                 )
-                dgl[j, rows, :] = (dh * a.astype(F32)).astype(BF16)
-                dul[j, rows, :] = (dh * b.astype(F32)).astype(BF16)
-                hl[j, rows, :] = h
+                s = jax.nn.sigmoid(g)
+                b = g * s
+                al[j, rows, :] = (u * s * (1.0 + g * (1.0 - s))).astype(BF16)
+                bl[j, rows, :] = b.astype(BF16)
+                hl[j, rows, :] = (b * u).astype(BF16)
             return 0
 
         lax.fori_loop(0, blocks, body, 0)
         for i in range(per):
-            block_row = c * per + i
-            j0, j1 = icol[0, block_row], icol[1, block_row]
-            q0, q1 = ocol[0, block_row], ocol[1, block_row]
-            left = jnp.concatenate([xnr[o, i, mine, :] for o in range(n_col)], axis=0).T
-            acc[0, i] = acc[0, i] + dot(left, jnp.concatenate([dgl[j0], dgl[j1]], axis=1))
-            acc[1, i] = acc[1, i] + dot(left, jnp.concatenate([dul[j0], dul[j1]], axis=1))
+            q0, q1 = ocol[0, c * per + i], ocol[1, c * per + i]
             left = jnp.concatenate([dyr[k, o, :, i * BLK : (i + 1) * BLK] for o in range(n_col)], axis=0).T
             acc[2, i] = acc[2, i] + dot(left, jnp.concatenate([hl[q0], hl[q1]], axis=1))
+            xnt[i] = jnp.concatenate([xnr[o, i, mine, :] for o in range(n_col)], axis=0).T
+
+    def grads(k):
+        for d in range(n_y):
+            dh_copy(k, column(d, 1), sibling, 0).wait_recv()
+
+        def body(j, _):
+            dh = jnp.concatenate([dhall[k, o, j] for o in range(n_col)], axis=0).astype(F32)
+            dgl[j] = (dh * al[j].astype(F32)).astype(BF16)
+            dul[j] = (dh * bl[j].astype(F32)).astype(BF16)
+            return 0
+
+        lax.fori_loop(0, blocks, body, 0, unroll=2)
+        for i in range(per):
+            j0, j1 = icol[0, c * per + i], icol[1, c * per + i]
+            acc[0, i] = acc[0, i] + dot(xnt[i], jnp.concatenate([dgl[j0], dgl[j1]], axis=1))
+            acc[1, i] = acc[1, i] + dot(xnt[i], jnp.concatenate([dul[j0], dul[j1]], axis=1))
 
     def own_grads(owner, emit):
         for i in range(per):
@@ -574,36 +580,44 @@
         send_factors()
         lax.fori_loop(1, n_col, send_xn, 0)
 
-    take_dy(0)
+    @pl.when(p == 0)
+    def _():
+        spread_factors()
+
+    for k in range(AHEAD):
+        take_dy(k)
 
     def step(s, _):
         @pl.when(s < CHUNKS)
         def _():
+            @pl.when(s < CHUNKS - AHEAD)
+            def _():
+                take_dy(s + AHEAD)
+
             products(s)
-
-            @pl.when(s < CHUNKS - 1)
-            def _():
-                take_dy(s + 1)
-
             back(s)
 
+        @pl.when(jnp.logical_and(s == lead, p > 0))
+        def _():
+            spread_factors()
+
         @pl.when(jnp.logical_and(s >= lead + 1, s < lead + 1 + CHUNKS))
         def _():
             grads(s - lead - 1)
 
         @pl.when(jnp.logical_and(s >= lead, s < lead + CHUNKS))
         def _():
-            down_part(s - lead)
+            prepare(s - lead)
             pass_on(s - lead)
 
-        @pl.when(jnp.logical_and(s >= 1, s < CHUNKS + 1))
-        def _():
-            finish(s - 1)
-
-        return 0
-
-    lead = jnp.where(p == 0, 1, jnp.where(by_factors, CHUNKS + 1, 3 * CHUNKS))
-    lax.fori_loop(0, 2 * CHUNKS + 2, step, 0)
+        @pl.when(jnp.logical_and(s >= LATE, s < CHUNKS + LATE))
+        def _():
+            finish(s - LATE)
+
+        return 0
+
+    lead = jnp.where(p == 0, FACTORS_LATE, jnp.where(by_factors, CHUNKS + LATE, 3 * CHUNKS))
+    lax.fori_loop(0, 2 * CHUNKS + LATE + 1, step, 0)
 
     @pl.when(jnp.logical_not(by_factors))
     def _():
@@ -718,7 +732,7 @@
             pltpu.VMEM((blocks, both, BLK), F32),
             pltpu.VMEM((blocks, both, BLK), F32),
             pltpu.VMEM((blocks, both, BLK), BF16),
-            pltpu.VMEM((max(n_col * 3 * blocks * both, (12 * n_y - 6) * 2 * rows), BLK), BF16),
+            pltpu.VMEM((max(n_col * 2 * blocks * both, (12 * n_y - 6) * 2 * rows), BLK), BF16),
             pltpu.VMEM((CHUNKS, n_col, blocks, small, BLK), BF16),
             pltpu.VMEM((blocks, both, BLK), BF16),
             pltpu.VMEM((blocks, both, BLK), BF16),
@@ -730,6 +744,9 @@
             pltpu.VMEM((blocks, n_col * small, BLK), BF16),
             pltpu.VMEM((blocks, n_col * small, BLK), BF16),
             pltpu.VMEM((blocks, n_col * small, BLK), BF16),
+            pltpu.VMEM((blocks, n_col * small, BLK), BF16),
+            pltpu.VMEM((blocks, n_col * small, BLK), BF16),
+            pltpu.VMEM((per, BLK, n_col * small), BF16),
             pltpu.VMEM((3, per, BLK, 2 * BLK), F32),
             pltpu.VMEM((8, BLK), jnp.int32),
             pltpu.SMEM((8, BLK), jnp.int32),

time: 156 us -> 140 us (0.90)
  Pallas kernels: 155 us -> 138 us
    pallas_call x1, Pallas kernels: 153 us -> 136 us  [local(): pl.pallas_call(functools.partial(main_kernel, sizes), out_shape=outs, in_...]
where the time goes in v3:
time: 140 us; the launch traced here: 139 us
  Pallas kernels  138 us (99%)
    pallas_call x1, Pallas kernels, local(): pl.pallas_call(functools.partial(main_kernel, sizes), out_shape=outs, in_...  136 us

profile of v3, /device:TPU:1, one launch (start us, length us, event | category | flops | bytes accessed | tf_op | source)
XLA Modules:
  0.0 138.6 jit_solution(1735458184140912715)
XLA Ops:
  0.6 135.8 %backward.1 = (bf16[128,512]{1,0:T(8,128)(2,1)}, bf16[512,256]{1,0:T(8,128)(2,1)}, bf16[512,256]{1,0:T(8,128)(2,1)}, bf16[512,256]{1,0:T(8,128)(2,1)}) custom-call(bf16[128,512]{1,0:T(8,128)(2,1)} %bitcast.20, bf16[128,512]{1,0:T(8,128)(2,1)} %bitcast.21, bf16[1,512]{1,0:T(2,128)(2,1)} %gain_ref.1, bf16[512,256]{1,0:T(8,128)(2,1)} %bitcast.17, ...), custom_call_target="tpu_custom_call" | custom-call | tf_op jit(solution)/shard_map/backward/pallas_call | solution.py:717
  136.4 2.1 %hand_over.1 = (bf16[128,512]{1,0:T(8,128)(2,1)}, bf16[512,256]{1,0:T(8,128)(2,1)}, bf16[512,256]{1,0:T(8,128)(2,1)}, bf16[512,256]{1,0:T(8,128)(2,1)}) custom-call(bf16[128,512]{1,0:T(8,128)(2,1)} %get-tuple-element.12.a, bf16[512,256]{1,0:T(8,128)(2,1)} %get-tuple-element.13.b, bf16[512,256]{1,0:T(8,128)(2,1)} %get-tuple-element.14.c, ...), custom_call_target="tpu_custom_call" | custom-call | tf_op jit(solution)/shard_map/hand_over/pallas_call | solution.py:773

commit v4 on v3

--- a/solution.py
+++ b/solution.py
@@ -19,6 +19,8 @@
 FACTOR_SECTIONS = 2
 AHEAD = 1
 LATE = 1
+SPREAD = 4
+FIRST_LATE = 2
 FACTORS_LATE = 2
 
 
@@ -176,6 +178,10 @@
     def ring_copy(which, k, target):
         return remote(pool.at[shares(2, which, k), :], pool.at[shares(3, which, k), :], ysend.at[which, k], yrecv.at[which, k], {"col": target})
 
+    def far_copy(which, h):
+        rows = [pl.ds(pl.multiple_of(share_start(part, which, 2) + h * block // 2, block // 2), block // 2) for part in (2, 3)]
+        return remote(pool.at[rows[0], :], pool.at[rows[1], :], ysend.at[which, 2 * h], yrecv.at[which, 2 * h], {"col": (up_y, down_y)[h]})
+
     def dh_copy(k, owner, target, number):
         return remote(dhall.at[k, owner], dhall.at[k, owner], dsend.at[k, number], drecv.at[k, owner], {"col": target})
 
@@ -538,36 +544,62 @@
     def get(part, which, k, i):
         return jnp.concatenate([pool[part_rows(part, which, k, i, s), :] for s in range(2)], axis=1).astype(F32)
 
-    def to_sibling(k, _):
+    def to_sibling(k):
         own_grads(lax.rem(y + k, n_y) * 2 + (1 - core), lambda which, i, value: put(0, which, k, i, value))
         for which in range(3):
             pair_copy(which, k).start()
-        return 0
-
-    def to_ring(step, _):
-        k = pick(step, (2, 1, 3, 0))
+
+    def to_ring(k):
         target = lax.rem(y + k, n_y) * 2 + core
         for which in range(3):
             pair_copy(which, k).wait_recv()
 
+        for h in range(2):
+
+            @pl.when(k == 2 * h + 1)
+            def _(h=h):
+                for which in range(3):
+                    far_copy(which, h).wait_recv()
+
         def emit(which, i, value):
-            value = value + get(1, which, k, i)
-            acc[which, i] = value
+            acc[which, i] = value + get(1, which, k, i)
+
+            @pl.when(k == (1 if i < per // 2 else 3))
+            def _():
+                acc[which, i] = acc[which, i] + get(3, which, 2, i)
 
             @pl.when(k > 0)
             def _():
-                put(2, which, k, i, value)
+                put(2, which, k, i, acc[which, i])
 
         own_grads(target, emit)
 
-        @pl.when(k > 0)
+        @pl.when(k == 2)
+        def _():
+            for which in range(3):
+                for h in range(2):
+                    far_copy(which, h).start()
+
+        @pl.when(lax.rem(k, 2) == 1)
         def _():
             for which in range(3):
                 ring_copy(which, k, target).start()
 
-        return 0
-
-    def collect(k, _):
+    def to_owners(s, _):
+        order = (2, 1, 3, 0)
+
+        @pl.when(s < n_y)
+        def _():
+            to_sibling(pick(s, order))
+
+        @pl.when(s >= 1)
+        def _():
+            to_ring(pick(s - 1, order))
+
+        return 0
+
+    def collect(side, _):
+        k = 2 * side + 1
         for which in range(3):
             ring_copy(which, k, sibling).wait_recv()
             for i in range(per):
@@ -597,10 +629,14 @@
             products(s)
             back(s)
 
-        @pl.when(jnp.logical_and(s == lead, p > 0))
+        @pl.when(jnp.logical_and(s == spread, jnp.logical_and(by_factors, p > 0)))
         def _():
             spread_factors()
 
+        @pl.when(jnp.logical_and(s >= lead, s < lead + CHUNKS))
+        def _():
+            pass_on(s - lead)
+
         @pl.when(jnp.logical_and(s >= lead + 1, s < lead + 1 + CHUNKS))
         def _():
             grads(s - lead - 1)
@@ -608,22 +644,22 @@
         @pl.when(jnp.logical_and(s >= lead, s < lead + CHUNKS))
         def _():
             prepare(s - lead)
-            pass_on(s - lead)
-
-        @pl.when(jnp.logical_and(s >= LATE, s < CHUNKS + LATE))
-        def _():
-            finish(s - LATE)
-
-        return 0
-
+
+        @pl.when(jnp.logical_and(s >= late, s < CHUNKS + late))
+        def _():
+            finish(s - late)
+
+        return 0
+
+    late = jnp.where(p == n_pipe - 1, FIRST_LATE, LATE)
+    spread = jnp.where(p == 1, SPREAD, CHUNKS + LATE)
     lead = jnp.where(p == 0, FACTORS_LATE, jnp.where(by_factors, CHUNKS + LATE, 3 * CHUNKS))
     lax.fori_loop(0, 2 * CHUNKS + LATE + 1, step, 0)
 
     @pl.when(jnp.logical_not(by_factors))
     def _():
-        lax.fori_loop(0, n_y, to_sibling, 0)
-        lax.fori_loop(0, n_y, to_ring, 0)
-        lax.fori_loop(1, n_y, collect, 0)
+        lax.fori_loop(0, n_y + 1, to_owners, 0)
+        lax.fori_loop(0, 2, collect, 0)
 
     for i in range(per):
         for which, (ref, cnt) in enumerate(((ggate_ref, icnt), (gup_ref, icnt), (gdown_ref, ocnt))):
@@ -669,8 +705,9 @@
         for which in range(3):
             for k in range(n_y):
                 pair_copy(which, k).wait_send()
-                if k > 0:
-                    ring_copy(which, k, sibling).wait_send()
+            for h in range(2):
+                far_copy(which, h).wait_send()
+                ring_copy(which, 2 * h + 1, sibling).wait_send()
 
     @pl.when(by_factors)
     def _():

time: 140 us -> 138 us (0.986)
  no operation moved by 1% of the time
where the time goes in v4:
time: 138 us; the launch traced here: 137 us
  Pallas kernels  137 us (99%)
    pallas_call x1, Pallas kernels, local(): pl.pallas_call(functools.partial(main_kernel, sizes), out_shape=outs, in_...  135 us

profile of v4, /device:TPU:1, one launch (start us, length us, event | category | flops | bytes accessed | tf_op | source)
XLA Modules:
  0.0 137.4 jit_solution(7503832168786822622)
XLA Ops:
  0.6 134.6 %backward.1 = (bf16[128,512]{1,0:T(8,128)(2,1)}, bf16[512,256]{1,0:T(8,128)(2,1)}, bf16[512,256]{1,0:T(8,128)(2,1)}, bf16[512,256]{1,0:T(8,128)(2,1)}) custom-call(bf16[128,512]{1,0:T(8,128)(2,1)} %bitcast.20, bf16[128,512]{1,0:T(8,128)(2,1)} %bitcast.21, bf16[1,512]{1,0:T(2,128)(2,1)} %gain_ref.1, bf16[512,256]{1,0:T(8,128)(2,1)} %bitcast.17, ...), custom_call_target="tpu_custom_call" | custom-call | tf_op jit(solution)/shard_map/backward/pallas_call | solution.py:754
  135.3 2.1 %hand_over.1 = (bf16[128,512]{1,0:T(8,128)(2,1)}, bf16[512,256]{1,0:T(8,128)(2,1)}, bf16[512,256]{1,0:T(8,128)(2,1)}, bf16[512,256]{1,0:T(8,128)(2,1)}) custom-call(bf16[128,512]{1,0:T(8,128)(2,1)} %get-tuple-element.12.a, bf16[512,256]{1,0:T(8,128)(2,1)} %get-tuple-element.13.b, bf16[512,256]{1,0:T(8,128)(2,1)} %get-tuple-element.14.c, ...), custom_call_target="tpu_custom_call" | custom-call | tf_op jit(solution)/shard_map/hand_over/pallas_call | solution.py:810

commit v5 on v4

--- a/solution.py
+++ b/solution.py
@@ -66,8 +66,8 @@
     x_ref, go_ref, gain_ref, gate_ref, up_ref, down_ref, icol_rows, ocol_rows,
     icol, icnt, ocol, ocnt,
     gin_ref, ggate_ref, gup_ref, gdown_ref,
-    wall, wt, xg, xn, rinv, pg, pu, sg, ab, bb, cb, hb, pool, dhall, dgb, dub, dyg, dyr, xnr, rss, rsr, al, bl, hl, dgl, dul, xnt, acc, tabv, tab,
-    tabsem, wsend, wrecv, xsend, xrecv, gsend, grecv, hsend, hrecv, rsend, rrecv,
+    wall, wt, xg, xn, rinv, pg, pu, sg, ab, bb, cb, hb, pool, dhall, dgb, dub, dyg, dyr, xnr, rss, rsr, al, bl, hl, dgl, dul, xnt, acc, tabv, tab, held,
+    heldsem, tabsem, wsend, wrecv, xsend, xrecv, gsend, grecv, hsend, hrecv, rsend, rrecv,
     asend, arecv, nsend, nrecv, dsend, drecv, csend, crecv, psend, precv, ysend, yrecv,
 ):
     n_pipe, n_row, n_y, blocks = sizes
@@ -118,13 +118,17 @@
         for row in (r, partner):
             pl.semaphore_signal(barrier, inc=1, device_id={"pipe": p + 1, "row": row}, device_id_type=MESH)
 
+    fetches = [pltpu.make_async_copy(src, held.at[i], heldsem.at[i]) for i, src in enumerate((gate_ref, up_ref, down_ref))]
+    for fetch in fetches:
+        fetch.start()
     xg[r, 0:both, :] = x_ref[...]
     xg[r, both : both + 16, :] = jnp.broadcast_to(gain_ref[...].astype(F32), (16, width)).astype(BF16)
-    for i in range(per):
-        for which, (ref, cnt) in enumerate(((gate_ref, icnt), (up_ref, icnt), (down_ref, ocnt))):
+    for which, cnt in enumerate((icnt, icnt, ocnt)):
+        fetches[which].wait()
+        for i in range(per):
             live = cnt[c * per + i]
             slot = lax.broadcasted_iota(jnp.int32, (BLK, 2 * BLK), 1) // BLK
-            value = ref[i * BLK : (i + 1) * BLK, :].astype(F32)
+            value = held[which, i * BLK : (i + 1) * BLK, :].astype(F32)
             wall[c, (i * 3 + which) * BLK : (i * 3 + which + 1) * BLK, :] = jnp.where(slot < live, value, 0.0).astype(BF16)
 
     @pl.when(p == n_pipe - 1)
@@ -192,11 +196,8 @@
         return remote(dyg.at[k, place(target)], dyr.at[k, source], csend.at[k, number], crecv.at[k, source], {"col": target})
 
     def send_dy(k):
-        def body(d, _):
+        for d in (2, 1, 3):
             dy_copy(k, x, lax.rem(x + d, n_x), d).start()
-            return 0
-
-        lax.fori_loop(1, n_x, body, 0)
 
     def send_x(d, _):
         x_copy(r, lax.rem(r + d, n_row), d).start()
@@ -359,7 +360,7 @@
 
     def products(k):
         def body(d, _):
-            from_x = lax.rem(x + d, n_x)
+            from_x = lax.rem(x + pick(d, (0, 1, 3, 2)), n_x)
 
             @pl.when(d > 0)
             def _():
@@ -754,7 +755,7 @@
     results = pl.pallas_call(
         functools.partial(main_kernel, sizes),
         out_shape=outs,
-        in_specs=[vmem] * 8 + [smem] * 4,
+        in_specs=[vmem] * 3 + [pl.BlockSpec(memory_space=pl.ANY)] * 3 + [vmem] * 2 + [smem] * 4,
         out_specs=[vmem] * 4,
         scratch_shapes=[
             pltpu.VMEM((n_col, 3 * rows, 2 * BLK), BF16),
@@ -787,6 +788,8 @@
             pltpu.VMEM((3, per, BLK, 2 * BLK), F32),
             pltpu.VMEM((8, BLK), jnp.int32),
             pltpu.SMEM((8, BLK), jnp.int32),
+            pltpu.VMEM((3, rows, 2 * BLK), BF16),
+            dma((3,)),
             dma,
             dma((28,)), dma((n_col, per)),
             dma((n_row,)), dma((n_row,)),

time: 138 us -> 137 us (level)
  no operation moved by 1% of the time
where the time goes in v5:
time: 137 us
  Pallas kernels  136 us (99%)
    pallas_call x1, Pallas kernels, local(): pl.pallas_call(functools.partial(main_kernel, sizes), out_shape=outs, in_...  134 us

profile of v5, /device:TPU:1, one launch (start us, length us, event | category | flops | bytes accessed | tf_op | source)
XLA Modules:
  0.0 136.5 jit_solution(18158070636321308881)
XLA Ops:
  0.6 133.8 %backward.1 = (bf16[128,512]{1,0:T(8,128)(2,1)}, bf16[512,256]{1,0:T(8,128)(2,1)}, bf16[512,256]{1,0:T(8,128)(2,1)}, bf16[512,256]{1,0:T(8,128)(2,1)}) custom-call(bf16[128,512]{1,0:T(8,128)(2,1)} %bitcast.20, bf16[128,512]{1,0:T(8,128)(2,1)} %bitcast.21, bf16[1,512]{1,0:T(2,128)(2,1)} %gain_ref.1, bf16[512,256]{1,0:T(8,128)(2,1)} %bitcast.17, ...), custom_call_target="tpu_custom_call" | custom-call | tf_op jit(solution)/shard_map/backward/pallas_call | solution.py:755
  134.4 2.1 %hand_over.1 = (bf16[128,512]{1,0:T(8,128)(2,1)}, bf16[512,256]{1,0:T(8,128)(2,1)}, bf16[512,256]{1,0:T(8,128)(2,1)}, bf16[512,256]{1,0:T(8,128)(2,1)}) custom-call(bf16[128,512]{1,0:T(8,128)(2,1)} %get-tuple-element.12.a, bf16[512,256]{1,0:T(8,128)(2,1)} %get-tuple-element.13.b, bf16[512,256]{1,0:T(8,128)(2,1)} %get-tuple-element.14.c, ...), custom_call_target="tpu_custom_call" | custom-call | tf_op jit(solution)/shard_map/hand_over/pallas_call | solution.py:813
